TPU v7x, 512 devices: a whole 4x8x8 slice. The times are simulated.
512 devices in a mesh: inner: 16 (over x, y_hi), outer: 8 (over z), head: 4 (over y_lo, core).
Axes of the slice: x: 4, y: 8 (y_hi: 4, y_lo: 2; y = y_hi * 2 + y_lo), z: 8, core: 2. Of those that a mesh axis runs over, the one named last changes fastest.
Arguments:
- queries: bfloat16 [16384, 24, 128], P(('outer', 'inner'), 'head'), may hold values from -6 to 6
- key_rows: bfloat16 [16384, 4, 128], P(('outer', 'inner'), 'head'), may hold values from -6 to 6
- value_rows: bfloat16 [16384, 4, 128], P(('outer', 'inner'), 'head'), may hold values from -6 to 6
- attn_out: bfloat16 [16384, 24, 128], P(('outer', 'inner'), 'head'), may hold values from -3 to 3
- grad_out: bfloat16 [16384, 24, 128], P(('outer', 'inner'), 'head'), may hold values from -96 to 96
- log_norms: float32 [24, 16384], P('head', ('outer', 'inner'))
- pair_order: int32 [16], replicated, may hold values from 0 to 15, each once
Outputs:
- grad_queries: bfloat16 [16384, 24, 128], P(('outer', 'inner'), 'head')
- grad_keys: bfloat16 [16384, 4, 128], P(('outer', 'inner'), 'head')
- grad_values: bfloat16 [16384, 4, 128], P(('outer', 'inner'), 'head')
Inputs may be any that keep to these rules, and one draw needn't show every extreme that they name: Index i of inner holds, in every segment, span pair_order[i] in its first 64 rows and span 32 - 1 - pair_order[i] in its last 64 rows.
All inputs are finite; a program needn't handle non-finite values.
Results may differ from a plain program's by a relative error of at most 0.0053.
Values may be sent and summed in bfloat16 or wider, within the bound.
A program may use at most 64 MiB of HBM per device.

v0:
```python
import math

import jax
import jax.numpy as jnp
from jax import lax
from jax.sharding import PartitionSpec as P


def from_behind(block, axis, distance):
    devices = range(lax.axis_size(axis))
    route = [((i - distance) % len(devices), i) for i in devices]
    return lax.ppermute(block, axis, route)


def passed_along(value, axis, steps):
    count = lax.axis_size(axis)
    initial, last = (max(0, -steps), min(count, count - steps))
    return lax.ppermute(value, axis, [(source, source + steps) for source in range(initial, last)])


def segment_positions(pair_order, within, span_rows):
    slot_index = within // (2 * span_rows)
    local_rows = within % (2 * span_rows)
    rank_value = jnp.take(pair_order, slot_index)
    span_count = 2 * pair_order.shape[0]
    first_half = rank_value * span_rows + local_rows
    second_half = (span_count - 1 - rank_value) * span_rows + local_rows - span_rows
    return jnp.where(local_rows < span_rows, first_half, second_half)


def block_grads(
    queries_five, grad_five, norms_four, dots_four, key_blocks, value_blocks, visible, inv_root
):
    scores = (
        jnp.einsum(
            "arhgd,bkhd->ahgrbk", queries_five, key_blocks, preferred_element_type=jnp.float32
        )
        * inv_root
    )
    attn_weights = jnp.where(
        visible[:, None, None], jnp.exp(scores - norms_four[..., None, None]), 0.0
    )
    weights_half = attn_weights.astype(jnp.bfloat16)
    grad_weights = jnp.einsum(
        "arhgd,bkhd->ahgrbk", grad_five, value_blocks, preferred_element_type=jnp.float32
    )
    grad_scores = (attn_weights * (grad_weights - dots_four[..., None, None])).astype(jnp.bfloat16)
    value_grad = jnp.einsum(
        "ahgrbk,arhgd->bkhd", weights_half, grad_five, preferred_element_type=jnp.float32
    )
    key_grad = (
        jnp.einsum(
            "ahgrbk,arhgd->bkhd", grad_scores, queries_five, preferred_element_type=jnp.float32
        )
        * inv_root
    )
    query_grad = (
        jnp.einsum(
            "ahgrbk,bkhd->arhgd", grad_scores, key_blocks, preferred_element_type=jnp.float32
        )
        * inv_root
    )
    return (query_grad, key_grad, value_grad)


def inner_lap(blocks, moving, resident, update):
    cycle_size = lax.axis_size("inner")
    my_index = lax.axis_index("inner")

    def one_turn(turn_index, state_tuple):
        blocks, moving, resident = state_tuple
        moving, resident = update(blocks, moving, resident, (my_index - turn_index) % cycle_size)
        blocks = from_behind(blocks, "inner", 1)
        moving = from_behind(moving, "inner", 1)
        return (blocks, moving, resident)

    blocks, moving, resident = lax.fori_loop(
        0, cycle_size - 1, one_turn, (blocks, moving, resident)
    )
    moving, resident = update(blocks, moving, resident, (my_index + 1) % cycle_size)
    moving = from_behind(moving, "inner", 1)
    return (moving, resident)


def on_device(queries, key_rows, value_rows, attn_out, grad_out, log_norms, pair_order):
    row_count, q_local, head_size = queries.shape
    kv_local = key_rows.shape[1]
    group_size = q_local // kv_local
    span_rows = row_count // 2
    inv_root = 1.0 / math.sqrt(head_size)
    my_index = lax.axis_index("inner")
    outer_index = lax.axis_index("outer")
    local_rows = jnp.arange(row_count, dtype=jnp.int32)

    def positions_of(slot_index):
        return segment_positions(pair_order, slot_index * row_count + local_rows, span_rows)

    my_positions = positions_of(my_index)
    row_dot = jnp.sum(grad_out.astype(jnp.float32) * attn_out.astype(jnp.float32), axis=-1).T
    own_pairs = jnp.stack([key_rows, value_rows])
    prev_pairs = passed_along(own_pairs, "outer", 1)
    has_prev = outer_index > 0
    query_five = queries.reshape(row_count, kv_local, group_size, head_size)[None]
    grad_five = grad_out.reshape(row_count, kv_local, group_size, head_size)[None]
    norms_four = log_norms.reshape(kv_local, group_size, row_count)[None]
    dots_four = row_dot.reshape(kv_local, group_size, row_count)[None]
    blocks = jnp.stack([own_pairs, prev_pairs])

    def update(blocks, moving, resident, source):
        key_positions = positions_of(source)
        causal = key_positions[None, :] <= my_positions[:, None]
        visible = jnp.stack([causal, jnp.broadcast_to(has_prev, causal.shape)], axis=1)[None]
        query_grad, key_grad, value_grad = block_grads(
            query_five,
            grad_five,
            norms_four,
            dots_four,
            blocks[:, 0],
            blocks[:, 1],
            visible,
            inv_root,
        )
        return (moving + jnp.stack([key_grad, value_grad], axis=1), resident + query_grad)

    moving = jnp.zeros(blocks.shape, jnp.float32)
    resident = jnp.zeros(query_five.shape, jnp.float32)
    moving, resident = inner_lap(blocks, moving, resident, update)
    returned = passed_along(moving[1], "outer", -1)
    pair_grads = moving[0] + returned
    query_total = resident[0]
    grad_queries = query_total.reshape(row_count, q_local, head_size).astype(jnp.bfloat16)
    return (grad_queries, pair_grads[0].astype(jnp.bfloat16), pair_grads[1].astype(jnp.bfloat16))


def solution(mesh):
    in_specs = (
        P(("outer", "inner"), "head", None),
        P(("outer", "inner"), "head", None),
        P(("outer", "inner"), "head", None),
        P(("outer", "inner"), "head", None),
        P(("outer", "inner"), "head", None),
        P("head", ("outer", "inner")),
        P(),
    )
    out_specs = (
        P(("outer", "inner"), "head", None),
        P(("outer", "inner"), "head", None),
        P(("outer", "inner"), "head", None),
    )
    return jax.shard_map(
        on_device, mesh=mesh, in_specs=in_specs, out_specs=out_specs, check_vma=False
    )
```

profile of v0, /device:TPU:204, one launch (start us, length us, event | category | flops | bytes accessed | tf_op | source)
XLA Modules:
  0.0 560.5 jit_solution(7973597947960354344)
XLA Ops:
  1.5 5.5 collective-permute-start.2
  8.4 10.0 %compare_select_fusion.53 = s32[128]{0:T(128)S(1)} fusion(s32[]{:T(128)} %bitcast.20, s32[]{:T(128)} %bitcast.19, s32[]{:T(128)} %bitcast.18, s32[]{:T(128)} %bitcast.17, s32[]{:T(128)} %bitcast.16, s32[]{:T(128)} %bitcast.15, s32[]{:T(128)} %bitcast.14, s32[]{:T(128)} %bitcast.13, s32[]{:T(128)} %bitcast.12, s32[]{:T(128)} %bitcast.11, s32[]{:T(128)} %bitcast.10, ...), kind=kLoop, calls=%fused_computation.139 | loop fusion | flops 8320 | bytes 580 | tf_op jit(solution)/shard_map/jit(_where)/select_n | solution.py:28
  18.3 10.0 %compare_select_fusion.52 = s32[128]{0:T(128)S(1)} fusion(s32[]{:T(128)} %bitcast.20, s32[]{:T(128)} %bitcast.19, s32[]{:T(128)} %bitcast.18, s32[]{:T(128)} %bitcast.17, s32[]{:T(128)} %bitcast.16, s32[]{:T(128)} %bitcast.15, s32[]{:T(128)} %bitcast.14, s32[]{:T(128)} %bitcast.13, s32[]{:T(128)} %bitcast.12, s32[]{:T(128)} %bitcast.11, s32[]{:T(128)} %bitcast.10, ...), kind=kLoop, calls=%fused_computation.136 | loop fusion | flops 8320 | bytes 580 | tf_op jit(solution)/shard_map/jit(_where)/select_n | solution.py:28
  30.5 505.6 %while.21 = (s32[]{:T(128)}, bf16[2,2,128,1,128]{4,2,0,3,1:T(8,128)(2,1)S(1)}, f32[2,2,128,1,128]{4,2,0,3,1:T(8,128)S(1)}, f32[1,128,1,6,128]{4,1,3,0,2:T(8,128)...) while((s32[]{:T(128)}, ...), condition=%wide.region_2.4_spmd.clone, body=%wide.region_1.3_spmd.clone.sunk | while | flops 253517968 | bytes 8300609 | solution.py:77
  31.3 10.0 %compare_select_fusion.61 = s32[128]{0:T(128)S(1)} fusion(s32[]{:T(128)} %bitcast.336, s32[]{:T(128)} %bitcast.337, s32[]{:T(128)} %bitcast.338, s32[]{:T(128)} %bitcast.339, s32[]{:T(128)} %bitcast.340, s32[]{:T(128)} %bitcast.341, s32[]{:T(128)} %bitcast.342, s32[]{:T(128)} %bitcast.343, s32[]{:T(128)} %bitcast.344, s32[]{:T(128)} %bitcast.345, ...), kind=kLoop, calls=%fused_computation.51.clone.1 | loop fusion | flops 8320 | bytes 580 | tf_op jit(solution)/shard_map/while/body/eval_jaxpr/jit(_where)/select_n | solution.py:28
  42.5 4.5 collective-permute-start.1
  47.0 4.8 collective-permute-start
  52.2 14.1 %collective-permute-done = bf16[2,2,128,1,128]{4,2,0,3,1:T(8,128)(2,1)S(1)} collective-permute-done((bf16[2,2,128,1,128]{4,2,0,3,1:T(8,128)(2,1)S(1)}, bf16[2,2,128,1,128]{4,2,0,3,1:T(8,128)(2,1)S(1)}, u32[]{:S(2)}, u32[]{:S(2)}) %collective-permute-start) | collective-permute-done | bytes 131104 | tf_op jit(solution)/shard_map/while/body/eval_jaxpr/ppermute | solution.py:12
  67.0 10.0 %compare_select_fusion.61 = s32[128]{0:T(128)S(1)} fusion(s32[]{:T(128)} %bitcast.336, s32[]{:T(128)} %bitcast.337, s32[]{:T(128)} %bitcast.338, s32[]{:T(128)} %bitcast.339, s32[]{:T(128)} %bitcast.340, s32[]{:T(128)} %bitcast.341, s32[]{:T(128)} %bitcast.342, s32[]{:T(128)} %bitcast.343, s32[]{:T(128)} %bitcast.344, s32[]{:T(128)} %bitcast.345, ...), kind=kLoop, calls=%fused_computation.51.clone.1 | loop fusion | flops 8320 | bytes 580 | tf_op jit(solution)/shard_map/while/body/eval_jaxpr/jit(_where)/select_n | solution.py:28
  78.2 2.4 collective-permute-start.1
  80.7 4.7 collective-permute-start
  85.8 13.8 %collective-permute-done = bf16[2,2,128,1,128]{4,2,0,3,1:T(8,128)(2,1)S(1)} collective-permute-done((bf16[2,2,128,1,128]{4,2,0,3,1:T(8,128)(2,1)S(1)}, bf16[2,2,128,1,128]{4,2,0,3,1:T(8,128)(2,1)S(1)}, u32[]{:S(2)}, u32[]{:S(2)}) %collective-permute-start) | collective-permute-done | bytes 131104 | tf_op jit(solution)/shard_map/while/body/eval_jaxpr/ppermute | solution.py:12
  100.4 10.0 %compare_select_fusion.61 = s32[128]{0:T(128)S(1)} fusion(s32[]{:T(128)} %bitcast.336, s32[]{:T(128)} %bitcast.337, s32[]{:T(128)} %bitcast.338, s32[]{:T(128)} %bitcast.339, s32[]{:T(128)} %bitcast.340, s32[]{:T(128)} %bitcast.341, s32[]{:T(128)} %bitcast.342, s32[]{:T(128)} %bitcast.343, s32[]{:T(128)} %bitcast.344, s32[]{:T(128)} %bitcast.345, ...), kind=kLoop, calls=%fused_computation.51.clone.1 | loop fusion | flops 8320 | bytes 580 | tf_op jit(solution)/shard_map/while/body/eval_jaxpr/jit(_where)/select_n | solution.py:28
  111.6 1.9 collective-permute-start.1
  113.5 1.9 collective-permute-start
  115.9 19.7 %collective-permute-done = bf16[2,2,128,1,128]{4,2,0,3,1:T(8,128)(2,1)S(1)} collective-permute-done((bf16[2,2,128,1,128]{4,2,0,3,1:T(8,128)(2,1)S(1)}, bf16[2,2,128,1,128]{4,2,0,3,1:T(8,128)(2,1)S(1)}, u32[]{:S(2)}, u32[]{:S(2)}) %collective-permute-start) | collective-permute-done | bytes 131104 | tf_op jit(solution)/shard_map/while/body/eval_jaxpr/ppermute | solution.py:12
  136.3 10.0 %compare_select_fusion.61 = s32[128]{0:T(128)S(1)} fusion(s32[]{:T(128)} %bitcast.336, s32[]{:T(128)} %bitcast.337, s32[]{:T(128)} %bitcast.338, s32[]{:T(128)} %bitcast.339, s32[]{:T(128)} %bitcast.340, s32[]{:T(128)} %bitcast.341, s32[]{:T(128)} %bitcast.342, s32[]{:T(128)} %bitcast.343, s32[]{:T(128)} %bitcast.344, s32[]{:T(128)} %bitcast.345, ...), kind=kLoop, calls=%fused_computation.51.clone.1 | loop fusion | flops 8320 | bytes 580 | tf_op jit(solution)/shard_map/while/body/eval_jaxpr/jit(_where)/select_n | solution.py:28
  147.5 1.9 collective-permute-start.1
  149.4 1.9 collective-permute-start
  151.7 16.9 %collective-permute-done = bf16[2,2,128,1,128]{4,2,0,3,1:T(8,128)(2,1)S(1)} collective-permute-done((bf16[2,2,128,1,128]{4,2,0,3,1:T(8,128)(2,1)S(1)}, bf16[2,2,128,1,128]{4,2,0,3,1:T(8,128)(2,1)S(1)}, u32[]{:S(2)}, u32[]{:S(2)}) %collective-permute-start) | collective-permute-done | bytes 131104 | tf_op jit(solution)/shard_map/while/body/eval_jaxpr/ppermute | solution.py:12
  169.4 10.0 %compare_select_fusion.61 = s32[128]{0:T(128)S(1)} fusion(s32[]{:T(128)} %bitcast.336, s32[]{:T(128)} %bitcast.337, s32[]{:T(128)} %bitcast.338, s32[]{:T(128)} %bitcast.339, s32[]{:T(128)} %bitcast.340, s32[]{:T(128)} %bitcast.341, s32[]{:T(128)} %bitcast.342, s32[]{:T(128)} %bitcast.343, s32[]{:T(128)} %bitcast.344, s32[]{:T(128)} %bitcast.345, ...), kind=kLoop, calls=%fused_computation.51.clone.1 | loop fusion | flops 8320 | bytes 580 | tf_op jit(solution)/shard_map/while/body/eval_jaxpr/jit(_where)/select_n | solution.py:28
  180.6 1.9 collective-permute-start.1
  182.5 1.9 collective-permute-start
  184.8 13.0 %collective-permute-done = bf16[2,2,128,1,128]{4,2,0,3,1:T(8,128)(2,1)S(1)} collective-permute-done((bf16[2,2,128,1,128]{4,2,0,3,1:T(8,128)(2,1)S(1)}, bf16[2,2,128,1,128]{4,2,0,3,1:T(8,128)(2,1)S(1)}, u32[]{:S(2)}, u32[]{:S(2)}) %collective-permute-start) | collective-permute-done | bytes 131104 | tf_op jit(solution)/shard_map/while/body/eval_jaxpr/ppermute | solution.py:12
  198.6 10.0 %compare_select_fusion.61 = s32[128]{0:T(128)S(1)} fusion(s32[]{:T(128)} %bitcast.336, s32[]{:T(128)} %bitcast.337, s32[]{:T(128)} %bitcast.338, s32[]{:T(128)} %bitcast.339, s32[]{:T(128)} %bitcast.340, s32[]{:T(128)} %bitcast.341, s32[]{:T(128)} %bitcast.342, s32[]{:T(128)} %bitcast.343, s32[]{:T(128)} %bitcast.344, s32[]{:T(128)} %bitcast.345, ...), kind=kLoop, calls=%fused_computation.51.clone.1 | loop fusion | flops 8320 | bytes 580 | tf_op jit(solution)/shard_map/while/body/eval_jaxpr/jit(_where)/select_n | solution.py:28
  209.8 5.3 collective-permute-start.1
  215.1 1.9 collective-permute-start
  217.4 13.5 %collective-permute-done = bf16[2,2,128,1,128]{4,2,0,3,1:T(8,128)(2,1)S(1)} collective-permute-done((bf16[2,2,128,1,128]{4,2,0,3,1:T(8,128)(2,1)S(1)}, bf16[2,2,128,1,128]{4,2,0,3,1:T(8,128)(2,1)S(1)}, u32[]{:S(2)}, u32[]{:S(2)}) %collective-permute-start) | collective-permute-done | bytes 131104 | tf_op jit(solution)/shard_map/while/body/eval_jaxpr/ppermute | solution.py:12
  231.6 10.0 %compare_select_fusion.61 = s32[128]{0:T(128)S(1)} fusion(s32[]{:T(128)} %bitcast.336, s32[]{:T(128)} %bitcast.337, s32[]{:T(128)} %bitcast.338, s32[]{:T(128)} %bitcast.339, s32[]{:T(128)} %bitcast.340, s32[]{:T(128)} %bitcast.341, s32[]{:T(128)} %bitcast.342, s32[]{:T(128)} %bitcast.343, s32[]{:T(128)} %bitcast.344, s32[]{:T(128)} %bitcast.345, ...), kind=kLoop, calls=%fused_computation.51.clone.1 | loop fusion | flops 8320 | bytes 580 | tf_op jit(solution)/shard_map/while/body/eval_jaxpr/jit(_where)/select_n | solution.py:28
  242.8 5.3 collective-permute-start.1
  248.1 1.9 collective-permute-start
  250.5 14.9 %collective-permute-done = bf16[2,2,128,1,128]{4,2,0,3,1:T(8,128)(2,1)S(1)} collective-permute-done((bf16[2,2,128,1,128]{4,2,0,3,1:T(8,128)(2,1)S(1)}, bf16[2,2,128,1,128]{4,2,0,3,1:T(8,128)(2,1)S(1)}, u32[]{:S(2)}, u32[]{:S(2)}) %collective-permute-start) | collective-permute-done | bytes 131104 | tf_op jit(solution)/shard_map/while/body/eval_jaxpr/ppermute | solution.py:12
  266.1 10.0 %compare_select_fusion.61 = s32[128]{0:T(128)S(1)} fusion(s32[]{:T(128)} %bitcast.336, s32[]{:T(128)} %bitcast.337, s32[]{:T(128)} %bitcast.338, s32[]{:T(128)} %bitcast.339, s32[]{:T(128)} %bitcast.340, s32[]{:T(128)} %bitcast.341, s32[]{:T(128)} %bitcast.342, s32[]{:T(128)} %bitcast.343, s32[]{:T(128)} %bitcast.344, s32[]{:T(128)} %bitcast.345, ...), kind=kLoop, calls=%fused_computation.51.clone.1 | loop fusion | flops 8320 | bytes 580 | tf_op jit(solution)/shard_map/while/body/eval_jaxpr/jit(_where)/select_n | solution.py:28
  277.3 3.0 collective-permute-start.1
  280.3 1.9 collective-permute-start
  282.6 17.6 %collective-permute-done = bf16[2,2,128,1,128]{4,2,0,3,1:T(8,128)(2,1)S(1)} collective-permute-done((bf16[2,2,128,1,128]{4,2,0,3,1:T(8,128)(2,1)S(1)}, bf16[2,2,128,1,128]{4,2,0,3,1:T(8,128)(2,1)S(1)}, u32[]{:S(2)}, u32[]{:S(2)}) %collective-permute-start) | collective-permute-done | bytes 131104 | tf_op jit(solution)/shard_map/while/body/eval_jaxpr/ppermute | solution.py:12
  300.9 10.0 %compare_select_fusion.61 = s32[128]{0:T(128)S(1)} fusion(s32[]{:T(128)} %bitcast.336, s32[]{:T(128)} %bitcast.337, s32[]{:T(128)} %bitcast.338, s32[]{:T(128)} %bitcast.339, s32[]{:T(128)} %bitcast.340, s32[]{:T(128)} %bitcast.341, s32[]{:T(128)} %bitcast.342, s32[]{:T(128)} %bitcast.343, s32[]{:T(128)} %bitcast.344, s32[]{:T(128)} %bitcast.345, ...), kind=kLoop, calls=%fused_computation.51.clone.1 | loop fusion | flops 8320 | bytes 580 | tf_op jit(solution)/shard_map/while/body/eval_jaxpr/jit(_where)/select_n | solution.py:28
  312.2 1.9 collective-permute-start.1
  314.1 1.9 collective-permute-start
  316.4 17.1 %collective-permute-done = bf16[2,2,128,1,128]{4,2,0,3,1:T(8,128)(2,1)S(1)} collective-permute-done((bf16[2,2,128,1,128]{4,2,0,3,1:T(8,128)(2,1)S(1)}, bf16[2,2,128,1,128]{4,2,0,3,1:T(8,128)(2,1)S(1)}, u32[]{:S(2)}, u32[]{:S(2)}) %collective-permute-start) | collective-permute-done | bytes 131104 | tf_op jit(solution)/shard_map/while/body/eval_jaxpr/ppermute | solution.py:12
  334.3 10.0 %compare_select_fusion.61 = s32[128]{0:T(128)S(1)} fusion(s32[]{:T(128)} %bitcast.336, s32[]{:T(128)} %bitcast.337, s32[]{:T(128)} %bitcast.338, s32[]{:T(128)} %bitcast.339, s32[]{:T(128)} %bitcast.340, s32[]{:T(128)} %bitcast.341, s32[]{:T(128)} %bitcast.342, s32[]{:T(128)} %bitcast.343, s32[]{:T(128)} %bitcast.344, s32[]{:T(128)} %bitcast.345, ...), kind=kLoop, calls=%fused_computation.51.clone.1 | loop fusion | flops 8320 | bytes 580 | tf_op jit(solution)/shard_map/while/body/eval_jaxpr/jit(_where)/select_n | solution.py:28
  345.5 2.3 collective-permute-start.1
  347.8 1.9 collective-permute-start
  350.1 17.0 %collective-permute-done = bf16[2,2,128,1,128]{4,2,0,3,1:T(8,128)(2,1)S(1)} collective-permute-done((bf16[2,2,128,1,128]{4,2,0,3,1:T(8,128)(2,1)S(1)}, bf16[2,2,128,1,128]{4,2,0,3,1:T(8,128)(2,1)S(1)}, u32[]{:S(2)}, u32[]{:S(2)}) %collective-permute-start) | collective-permute-done | bytes 131104 | tf_op jit(solution)/shard_map/while/body/eval_jaxpr/ppermute | solution.py:12
  367.9 10.0 %compare_select_fusion.61 = s32[128]{0:T(128)S(1)} fusion(s32[]{:T(128)} %bitcast.336, s32[]{:T(128)} %bitcast.337, s32[]{:T(128)} %bitcast.338, s32[]{:T(128)} %bitcast.339, s32[]{:T(128)} %bitcast.340, s32[]{:T(128)} %bitcast.341, s32[]{:T(128)} %bitcast.342, s32[]{:T(128)} %bitcast.343, s32[]{:T(128)} %bitcast.344, s32[]{:T(128)} %bitcast.345, ...), kind=kLoop, calls=%fused_computation.51.clone.1 | loop fusion | flops 8320 | bytes 580 | tf_op jit(solution)/shard_map/while/body/eval_jaxpr/jit(_where)/select_n | solution.py:28
  379.1 1.9 collective-permute-start.1
  381.0 1.9 collective-permute-start
  383.3 14.8 %collective-permute-done = bf16[2,2,128,1,128]{4,2,0,3,1:T(8,128)(2,1)S(1)} collective-permute-done((bf16[2,2,128,1,128]{4,2,0,3,1:T(8,128)(2,1)S(1)}, bf16[2,2,128,1,128]{4,2,0,3,1:T(8,128)(2,1)S(1)}, u32[]{:S(2)}, u32[]{:S(2)}) %collective-permute-start) | collective-permute-done | bytes 131104 | tf_op jit(solution)/shard_map/while/body/eval_jaxpr/ppermute | solution.py:12
  398.8 10.0 %compare_select_fusion.61 = s32[128]{0:T(128)S(1)} fusion(s32[]{:T(128)} %bitcast.336, s32[]{:T(128)} %bitcast.337, s32[]{:T(128)} %bitcast.338, s32[]{:T(128)} %bitcast.339, s32[]{:T(128)} %bitcast.340, s32[]{:T(128)} %bitcast.341, s32[]{:T(128)} %bitcast.342, s32[]{:T(128)} %bitcast.343, s32[]{:T(128)} %bitcast.344, s32[]{:T(128)} %bitcast.345, ...), kind=kLoop, calls=%fused_computation.51.clone.1 | loop fusion | flops 8320 | bytes 580 | tf_op jit(solution)/shard_map/while/body/eval_jaxpr/jit(_where)/select_n | solution.py:28
  410.1 2.6 collective-permute-start.1
  412.7 1.9 collective-permute-start
  415.0 16.7 %collective-permute-done = bf16[2,2,128,1,128]{4,2,0,3,1:T(8,128)(2,1)S(1)} collective-permute-done((bf16[2,2,128,1,128]{4,2,0,3,1:T(8,128)(2,1)S(1)}, bf16[2,2,128,1,128]{4,2,0,3,1:T(8,128)(2,1)S(1)}, u32[]{:S(2)}, u32[]{:S(2)}) %collective-permute-start) | collective-permute-done | bytes 131104 | tf_op jit(solution)/shard_map/while/body/eval_jaxpr/ppermute | solution.py:12
  432.5 10.0 %compare_select_fusion.61 = s32[128]{0:T(128)S(1)} fusion(s32[]{:T(128)} %bitcast.336, s32[]{:T(128)} %bitcast.337, s32[]{:T(128)} %bitcast.338, s32[]{:T(128)} %bitcast.339, s32[]{:T(128)} %bitcast.340, s32[]{:T(128)} %bitcast.341, s32[]{:T(128)} %bitcast.342, s32[]{:T(128)} %bitcast.343, s32[]{:T(128)} %bitcast.344, s32[]{:T(128)} %bitcast.345, ...), kind=kLoop, calls=%fused_computation.51.clone.1 | loop fusion | flops 8320 | bytes 580 | tf_op jit(solution)/shard_map/while/body/eval_jaxpr/jit(_where)/select_n | solution.py:28
  443.7 3.1 collective-permute-start.1
  446.8 1.9 collective-permute-start
  449.1 17.0 %collective-permute-done = bf16[2,2,128,1,128]{4,2,0,3,1:T(8,128)(2,1)S(1)} collective-permute-done((bf16[2,2,128,1,128]{4,2,0,3,1:T(8,128)(2,1)S(1)}, bf16[2,2,128,1,128]{4,2,0,3,1:T(8,128)(2,1)S(1)}, u32[]{:S(2)}, u32[]{:S(2)}) %collective-permute-start) | collective-permute-done | bytes 131104 | tf_op jit(solution)/shard_map/while/body/eval_jaxpr/ppermute | solution.py:12
  466.9 10.0 %compare_select_fusion.61 = s32[128]{0:T(128)S(1)} fusion(s32[]{:T(128)} %bitcast.336, s32[]{:T(128)} %bitcast.337, s32[]{:T(128)} %bitcast.338, s32[]{:T(128)} %bitcast.339, s32[]{:T(128)} %bitcast.340, s32[]{:T(128)} %bitcast.341, s32[]{:T(128)} %bitcast.342, s32[]{:T(128)} %bitcast.343, s32[]{:T(128)} %bitcast.344, s32[]{:T(128)} %bitcast.345, ...), kind=kLoop, calls=%fused_computation.51.clone.1 | loop fusion | flops 8320 | bytes 580 | tf_op jit(solution)/shard_map/while/body/eval_jaxpr/jit(_where)/select_n | solution.py:28
  480.0 1.9 collective-permute-start
  482.3 17.7 %collective-permute-done = bf16[2,2,128,1,128]{4,2,0,3,1:T(8,128)(2,1)S(1)} collective-permute-done((bf16[2,2,128,1,128]{4,2,0,3,1:T(8,128)(2,1)S(1)}, bf16[2,2,128,1,128]{4,2,0,3,1:T(8,128)(2,1)S(1)}, u32[]{:S(2)}, u32[]{:S(2)}) %collective-permute-start) | collective-permute-done | bytes 131104 | tf_op jit(solution)/shard_map/while/body/eval_jaxpr/ppermute | solution.py:12
  500.7 10.0 %compare_select_fusion.61 = s32[128]{0:T(128)S(1)} fusion(s32[]{:T(128)} %bitcast.336, s32[]{:T(128)} %bitcast.337, s32[]{:T(128)} %bitcast.338, s32[]{:T(128)} %bitcast.339, s32[]{:T(128)} %bitcast.340, s32[]{:T(128)} %bitcast.341, s32[]{:T(128)} %bitcast.342, s32[]{:T(128)} %bitcast.343, s32[]{:T(128)} %bitcast.344, s32[]{:T(128)} %bitcast.345, ...), kind=kLoop, calls=%fused_computation.51.clone.1 | loop fusion | flops 8320 | bytes 580 | tf_op jit(solution)/shard_map/while/body/eval_jaxpr/jit(_where)/select_n | solution.py:28
  516.2 19.9 %collective-permute-done = bf16[2,2,128,1,128]{4,2,0,3,1:T(8,128)(2,1)S(1)} collective-permute-done((bf16[2,2,128,1,128]{4,2,0,3,1:T(8,128)(2,1)S(1)}, bf16[2,2,128,1,128]{4,2,0,3,1:T(8,128)(2,1)S(1)}, u32[]{:S(2)}, u32[]{:S(2)}) %collective-permute-start) | collective-permute-done | bytes 131104 | tf_op jit(solution)/shard_map/while/body/eval_jaxpr/ppermute | solution.py:12
  537.3 1.9 collective-permute-start.3
  539.4 12.4 %collective-permute-done.3 = f32[2,2,128,1,128]{4,2,0,3,1:T(8,128)S(1)} collective-permute-done((f32[2,2,128,1,128]{4,2,0,3,1:T(8,128)S(1)}, f32[2,2,128,1,128]{4,2,0,3,1:T(8,128)S(1)}, u32[]{:S(2)}, u32[]{:S(2)}) %collective-permute-start.3) | collective-permute-done | bytes 262176 | tf_op jit(solution)/shard_map/ppermute | solution.py:12
  554.8 5.1 collective-permute-done.4
  (197 shorter events, 49.9 us)
Async XLA Ops:
  0.6 27.8 %copy-start = (bf16[128,6,128]{2,0,1:T(8,128)(2,1)S(1)}, bf16[128,6,128]{2,0,1:T(8,128)(2,1)}, u32[]{:S(2)}) copy-start(bf16[128,6,128]{2,0,1:T(8,128)(2,1)} %param.15) | copy-start | bytes 589828
  1.5 28.1 %collective-permute-start.2 = (bf16[2,128,1,128]{3,1,0,2:T(8,128)(2,1)S(1)}, bf16[2,128,1,128]{3,1,0,2:T(8,128)(2,1)S(1)}, u32[]{:S(2)}, u32[]{:S(2)}) collective-permute-start(bf16[2,128,1,128]{3,1,0,2:T(8,128)(2,1)S(1)} %get-tuple-element.451), channel_id=1, source_target_pairs={{0,4},{4,8},{8,12},{12,16},{16,20},{20,24},{24,28},{1,5},{5,9},{9,... | collective-permute-start | bytes 196616 | tf_op jit(solution)/shard_map/ppermute | solution.py:18
  7.0 0.7 copy-start.2
  29.6 0.9 copy-start.1
  29.6 0.9 copy-start.3
  42.5 23.8 %collective-permute-start.1 = (f32[2,2,128,1,128]{4,2,0,3,1:T(8,128)S(1)}, f32[2,2,128,1,128]{4,2,0,3,1:T(8,128)S(1)}, u32[]{:S(2)}, u32[]{:S(2)}) collective-permute-start(f32[2,2,128,1,128]{4,2,0,3,1:T(8,128)S(1)} %maximum_add_fusion.3), channel_id=1, source_target_pairs={{480,0},{0,32},{32,64},{64,96},{96,128},{128,160},{160,192},{192,2... | collective-permute-start | bytes 786440 | tf_op jit(solution)/shard_map/while/body/eval_jaxpr/ppermute | solution.py:12
  47.0 19.3 %collective-permute-start = (bf16[2,2,128,1,128]{4,2,0,3,1:T(8,128)(2,1)S(1)}, bf16[2,2,128,1,128]{4,2,0,3,1:T(8,128)(2,1)S(1)}, u32[]{:S(2)}, u32[]{:S(2)}) collective-permute-start(bf16[2,2,128,1,128]{4,2,0,3,1:T(8,128)(2,1)S(1)} %copy.37), channel_id=1, source_target_pairs={{480,0},{0,32},{32,64},{64,96},{96,128},{128,160},{160,192},{192,2... | collective-permute-start | bytes 393224 | tf_op jit(solution)/shard_map/while/body/eval_jaxpr/ppermute | solution.py:12
  78.2 21.4 %collective-permute-start.1 = (f32[2,2,128,1,128]{4,2,0,3,1:T(8,128)S(1)}, f32[2,2,128,1,128]{4,2,0,3,1:T(8,128)S(1)}, u32[]{:S(2)}, u32[]{:S(2)}) collective-permute-start(f32[2,2,128,1,128]{4,2,0,3,1:T(8,128)S(1)} %maximum_add_fusion.3), channel_id=1, source_target_pairs={{480,0},{0,32},{32,64},{64,96},{96,128},{128,160},{160,192},{192,2... | collective-permute-start | bytes 786440 | tf_op jit(solution)/shard_map/while/body/eval_jaxpr/ppermute | solution.py:12
  80.7 19.0 %collective-permute-start = (bf16[2,2,128,1,128]{4,2,0,3,1:T(8,128)(2,1)S(1)}, bf16[2,2,128,1,128]{4,2,0,3,1:T(8,128)(2,1)S(1)}, u32[]{:S(2)}, u32[]{:S(2)}) collective-permute-start(bf16[2,2,128,1,128]{4,2,0,3,1:T(8,128)(2,1)S(1)} %copy.37), channel_id=1, source_target_pairs={{480,0},{0,32},{32,64},{64,96},{96,128},{128,160},{160,192},{192,2... | collective-permute-start | bytes 393224 | tf_op jit(solution)/shard_map/while/body/eval_jaxpr/ppermute | solution.py:12
  111.6 23.9 %collective-permute-start.1 = (f32[2,2,128,1,128]{4,2,0,3,1:T(8,128)S(1)}, f32[2,2,128,1,128]{4,2,0,3,1:T(8,128)S(1)}, u32[]{:S(2)}, u32[]{:S(2)}) collective-permute-start(f32[2,2,128,1,128]{4,2,0,3,1:T(8,128)S(1)} %maximum_add_fusion.3), channel_id=1, source_target_pairs={{480,0},{0,32},{32,64},{64,96},{96,128},{128,160},{160,192},{192,2... | collective-permute-start | bytes 786440 | tf_op jit(solution)/shard_map/while/body/eval_jaxpr/ppermute | solution.py:12
  113.5 22.0 %collective-permute-start = (bf16[2,2,128,1,128]{4,2,0,3,1:T(8,128)(2,1)S(1)}, bf16[2,2,128,1,128]{4,2,0,3,1:T(8,128)(2,1)S(1)}, u32[]{:S(2)}, u32[]{:S(2)}) collective-permute-start(bf16[2,2,128,1,128]{4,2,0,3,1:T(8,128)(2,1)S(1)} %copy.37), channel_id=1, source_target_pairs={{480,0},{0,32},{32,64},{64,96},{96,128},{128,160},{160,192},{192,2... | collective-permute-start | bytes 393224 | tf_op jit(solution)/shard_map/while/body/eval_jaxpr/ppermute | solution.py:12
  147.5 21.1 %collective-permute-start.1 = (f32[2,2,128,1,128]{4,2,0,3,1:T(8,128)S(1)}, f32[2,2,128,1,128]{4,2,0,3,1:T(8,128)S(1)}, u32[]{:S(2)}, u32[]{:S(2)}) collective-permute-start(f32[2,2,128,1,128]{4,2,0,3,1:T(8,128)S(1)} %maximum_add_fusion.3), channel_id=1, source_target_pairs={{480,0},{0,32},{32,64},{64,96},{96,128},{128,160},{160,192},{192,2... | collective-permute-start | bytes 786440 | tf_op jit(solution)/shard_map/while/body/eval_jaxpr/ppermute | solution.py:12
  149.4 19.2 %collective-permute-start = (bf16[2,2,128,1,128]{4,2,0,3,1:T(8,128)(2,1)S(1)}, bf16[2,2,128,1,128]{4,2,0,3,1:T(8,128)(2,1)S(1)}, u32[]{:S(2)}, u32[]{:S(2)}) collective-permute-start(bf16[2,2,128,1,128]{4,2,0,3,1:T(8,128)(2,1)S(1)} %copy.37), channel_id=1, source_target_pairs={{480,0},{0,32},{32,64},{64,96},{96,128},{128,160},{160,192},{192,2... | collective-permute-start | bytes 393224 | tf_op jit(solution)/shard_map/while/body/eval_jaxpr/ppermute | solution.py:12
  180.6 17.3 %collective-permute-start.1 = (f32[2,2,128,1,128]{4,2,0,3,1:T(8,128)S(1)}, f32[2,2,128,1,128]{4,2,0,3,1:T(8,128)S(1)}, u32[]{:S(2)}, u32[]{:S(2)}) collective-permute-start(f32[2,2,128,1,128]{4,2,0,3,1:T(8,128)S(1)} %maximum_add_fusion.3), channel_id=1, source_target_pairs={{480,0},{0,32},{32,64},{64,96},{96,128},{128,160},{160,192},{192,2... | collective-permute-start | bytes 786440 | tf_op jit(solution)/shard_map/while/body/eval_jaxpr/ppermute | solution.py:12
  182.5 15.3 %collective-permute-start = (bf16[2,2,128,1,128]{4,2,0,3,1:T(8,128)(2,1)S(1)}, bf16[2,2,128,1,128]{4,2,0,3,1:T(8,128)(2,1)S(1)}, u32[]{:S(2)}, u32[]{:S(2)}) collective-permute-start(bf16[2,2,128,1,128]{4,2,0,3,1:T(8,128)(2,1)S(1)} %copy.37), channel_id=1, source_target_pairs={{480,0},{0,32},{32,64},{64,96},{96,128},{128,160},{160,192},{192,2... | collective-permute-start | bytes 393224 | tf_op jit(solution)/shard_map/while/body/eval_jaxpr/ppermute | solution.py:12
  209.8 21.1 %collective-permute-start.1 = (f32[2,2,128,1,128]{4,2,0,3,1:T(8,128)S(1)}, f32[2,2,128,1,128]{4,2,0,3,1:T(8,128)S(1)}, u32[]{:S(2)}, u32[]{:S(2)}) collective-permute-start(f32[2,2,128,1,128]{4,2,0,3,1:T(8,128)S(1)} %maximum_add_fusion.3), channel_id=1, source_target_pairs={{480,0},{0,32},{32,64},{64,96},{96,128},{128,160},{160,192},{192,2... | collective-permute-start | bytes 786440 | tf_op jit(solution)/shard_map/while/body/eval_jaxpr/ppermute | solution.py:12
  215.1 15.8 %collective-permute-start = (bf16[2,2,128,1,128]{4,2,0,3,1:T(8,128)(2,1)S(1)}, bf16[2,2,128,1,128]{4,2,0,3,1:T(8,128)(2,1)S(1)}, u32[]{:S(2)}, u32[]{:S(2)}) collective-permute-start(bf16[2,2,128,1,128]{4,2,0,3,1:T(8,128)(2,1)S(1)} %copy.37), channel_id=1, source_target_pairs={{480,0},{0,32},{32,64},{64,96},{96,128},{128,160},{160,192},{192,2... | collective-permute-start | bytes 393224 | tf_op jit(solution)/shard_map/while/body/eval_jaxpr/ppermute | solution.py:12
  242.8 22.5 %collective-permute-start.1 = (f32[2,2,128,1,128]{4,2,0,3,1:T(8,128)S(1)}, f32[2,2,128,1,128]{4,2,0,3,1:T(8,128)S(1)}, u32[]{:S(2)}, u32[]{:S(2)}) collective-permute-start(f32[2,2,128,1,128]{4,2,0,3,1:T(8,128)S(1)} %maximum_add_fusion.3), channel_id=1, source_target_pairs={{480,0},{0,32},{32,64},{64,96},{96,128},{128,160},{160,192},{192,2... | collective-permute-start | bytes 786440 | tf_op jit(solution)/shard_map/while/body/eval_jaxpr/ppermute | solution.py:12
  248.1 17.2 %collective-permute-start = (bf16[2,2,128,1,128]{4,2,0,3,1:T(8,128)(2,1)S(1)}, bf16[2,2,128,1,128]{4,2,0,3,1:T(8,128)(2,1)S(1)}, u32[]{:S(2)}, u32[]{:S(2)}) collective-permute-start(bf16[2,2,128,1,128]{4,2,0,3,1:T(8,128)(2,1)S(1)} %copy.37), channel_id=1, source_target_pairs={{480,0},{0,32},{32,64},{64,96},{96,128},{128,160},{160,192},{192,2... | collective-permute-start | bytes 393224 | tf_op jit(solution)/shard_map/while/body/eval_jaxpr/ppermute | solution.py:12
  277.3 22.9 %collective-permute-start.1 = (f32[2,2,128,1,128]{4,2,0,3,1:T(8,128)S(1)}, f32[2,2,128,1,128]{4,2,0,3,1:T(8,128)S(1)}, u32[]{:S(2)}, u32[]{:S(2)}) collective-permute-start(f32[2,2,128,1,128]{4,2,0,3,1:T(8,128)S(1)} %maximum_add_fusion.3), channel_id=1, source_target_pairs={{480,0},{0,32},{32,64},{64,96},{96,128},{128,160},{160,192},{192,2... | collective-permute-start | bytes 786440 | tf_op jit(solution)/shard_map/while/body/eval_jaxpr/ppermute | solution.py:12
  280.3 19.9 %collective-permute-start = (bf16[2,2,128,1,128]{4,2,0,3,1:T(8,128)(2,1)S(1)}, bf16[2,2,128,1,128]{4,2,0,3,1:T(8,128)(2,1)S(1)}, u32[]{:S(2)}, u32[]{:S(2)}) collective-permute-start(bf16[2,2,128,1,128]{4,2,0,3,1:T(8,128)(2,1)S(1)} %copy.37), channel_id=1, source_target_pairs={{480,0},{0,32},{32,64},{64,96},{96,128},{128,160},{160,192},{192,2... | collective-permute-start | bytes 393224 | tf_op jit(solution)/shard_map/while/body/eval_jaxpr/ppermute | solution.py:12
  312.2 21.4 %collective-permute-start.1 = (f32[2,2,128,1,128]{4,2,0,3,1:T(8,128)S(1)}, f32[2,2,128,1,128]{4,2,0,3,1:T(8,128)S(1)}, u32[]{:S(2)}, u32[]{:S(2)}) collective-permute-start(f32[2,2,128,1,128]{4,2,0,3,1:T(8,128)S(1)} %maximum_add_fusion.3), channel_id=1, source_target_pairs={{480,0},{0,32},{32,64},{64,96},{96,128},{128,160},{160,192},{192,2... | collective-permute-start | bytes 786440 | tf_op jit(solution)/shard_map/while/body/eval_jaxpr/ppermute | solution.py:12
  314.1 19.5 %collective-permute-start = (bf16[2,2,128,1,128]{4,2,0,3,1:T(8,128)(2,1)S(1)}, bf16[2,2,128,1,128]{4,2,0,3,1:T(8,128)(2,1)S(1)}, u32[]{:S(2)}, u32[]{:S(2)}) collective-permute-start(bf16[2,2,128,1,128]{4,2,0,3,1:T(8,128)(2,1)S(1)} %copy.37), channel_id=1, source_target_pairs={{480,0},{0,32},{32,64},{64,96},{96,128},{128,160},{160,192},{192,2... | collective-permute-start | bytes 393224 | tf_op jit(solution)/shard_map/while/body/eval_jaxpr/ppermute | solution.py:12
  345.5 21.6 %collective-permute-start.1 = (f32[2,2,128,1,128]{4,2,0,3,1:T(8,128)S(1)}, f32[2,2,128,1,128]{4,2,0,3,1:T(8,128)S(1)}, u32[]{:S(2)}, u32[]{:S(2)}) collective-permute-start(f32[2,2,128,1,128]{4,2,0,3,1:T(8,128)S(1)} %maximum_add_fusion.3), channel_id=1, source_target_pairs={{480,0},{0,32},{32,64},{64,96},{96,128},{128,160},{160,192},{192,2... | collective-permute-start | bytes 786440 | tf_op jit(solution)/shard_map/while/body/eval_jaxpr/ppermute | solution.py:12
  347.8 19.3 %collective-permute-start = (bf16[2,2,128,1,128]{4,2,0,3,1:T(8,128)(2,1)S(1)}, bf16[2,2,128,1,128]{4,2,0,3,1:T(8,128)(2,1)S(1)}, u32[]{:S(2)}, u32[]{:S(2)}) collective-permute-start(bf16[2,2,128,1,128]{4,2,0,3,1:T(8,128)(2,1)S(1)} %copy.37), channel_id=1, source_target_pairs={{480,0},{0,32},{32,64},{64,96},{96,128},{128,160},{160,192},{192,2... | collective-permute-start | bytes 393224 | tf_op jit(solution)/shard_map/while/body/eval_jaxpr/ppermute | solution.py:12
  379.1 19.0 %collective-permute-start.1 = (f32[2,2,128,1,128]{4,2,0,3,1:T(8,128)S(1)}, f32[2,2,128,1,128]{4,2,0,3,1:T(8,128)S(1)}, u32[]{:S(2)}, u32[]{:S(2)}) collective-permute-start(f32[2,2,128,1,128]{4,2,0,3,1:T(8,128)S(1)} %maximum_add_fusion.3), channel_id=1, source_target_pairs={{480,0},{0,32},{32,64},{64,96},{96,128},{128,160},{160,192},{192,2... | collective-permute-start | bytes 786440 | tf_op jit(solution)/shard_map/while/body/eval_jaxpr/ppermute | solution.py:12
  381.0 17.1 %collective-permute-start = (bf16[2,2,128,1,128]{4,2,0,3,1:T(8,128)(2,1)S(1)}, bf16[2,2,128,1,128]{4,2,0,3,1:T(8,128)(2,1)S(1)}, u32[]{:S(2)}, u32[]{:S(2)}) collective-permute-start(bf16[2,2,128,1,128]{4,2,0,3,1:T(8,128)(2,1)S(1)} %copy.37), channel_id=1, source_target_pairs={{480,0},{0,32},{32,64},{64,96},{96,128},{128,160},{160,192},{192,2... | collective-permute-start | bytes 393224 | tf_op jit(solution)/shard_map/while/body/eval_jaxpr/ppermute | solution.py:12
  410.1 21.7 %collective-permute-start.1 = (f32[2,2,128,1,128]{4,2,0,3,1:T(8,128)S(1)}, f32[2,2,128,1,128]{4,2,0,3,1:T(8,128)S(1)}, u32[]{:S(2)}, u32[]{:S(2)}) collective-permute-start(f32[2,2,128,1,128]{4,2,0,3,1:T(8,128)S(1)} %maximum_add_fusion.3), channel_id=1, source_target_pairs={{480,0},{0,32},{32,64},{64,96},{96,128},{128,160},{160,192},{192,2... | collective-permute-start | bytes 786440 | tf_op jit(solution)/shard_map/while/body/eval_jaxpr/ppermute | solution.py:12
  412.7 19.1 %collective-permute-start = (bf16[2,2,128,1,128]{4,2,0,3,1:T(8,128)(2,1)S(1)}, bf16[2,2,128,1,128]{4,2,0,3,1:T(8,128)(2,1)S(1)}, u32[]{:S(2)}, u32[]{:S(2)}) collective-permute-start(bf16[2,2,128,1,128]{4,2,0,3,1:T(8,128)(2,1)S(1)} %copy.37), channel_id=1, source_target_pairs={{480,0},{0,32},{32,64},{64,96},{96,128},{128,160},{160,192},{192,2... | collective-permute-start | bytes 393224 | tf_op jit(solution)/shard_map/while/body/eval_jaxpr/ppermute | solution.py:12
  443.7 22.4 %collective-permute-start.1 = (f32[2,2,128,1,128]{4,2,0,3,1:T(8,128)S(1)}, f32[2,2,128,1,128]{4,2,0,3,1:T(8,128)S(1)}, u32[]{:S(2)}, u32[]{:S(2)}) collective-permute-start(f32[2,2,128,1,128]{4,2,0,3,1:T(8,128)S(1)} %maximum_add_fusion.3), channel_id=1, source_target_pairs={{480,0},{0,32},{32,64},{64,96},{96,128},{128,160},{160,192},{192,2... | collective-permute-start | bytes 786440 | tf_op jit(solution)/shard_map/while/body/eval_jaxpr/ppermute | solution.py:12
  446.8 19.3 %collective-permute-start = (bf16[2,2,128,1,128]{4,2,0,3,1:T(8,128)(2,1)S(1)}, bf16[2,2,128,1,128]{4,2,0,3,1:T(8,128)(2,1)S(1)}, u32[]{:S(2)}, u32[]{:S(2)}) collective-permute-start(bf16[2,2,128,1,128]{4,2,0,3,1:T(8,128)(2,1)S(1)} %copy.37), channel_id=1, source_target_pairs={{480,0},{0,32},{32,64},{64,96},{96,128},{128,160},{160,192},{192,2... | collective-permute-start | bytes 393224 | tf_op jit(solution)/shard_map/while/body/eval_jaxpr/ppermute | solution.py:12
  478.1 21.9 %collective-permute-start.1 = (f32[2,2,128,1,128]{4,2,0,3,1:T(8,128)S(1)}, f32[2,2,128,1,128]{4,2,0,3,1:T(8,128)S(1)}, u32[]{:S(2)}, u32[]{:S(2)}) collective-permute-start(f32[2,2,128,1,128]{4,2,0,3,1:T(8,128)S(1)} %maximum_add_fusion.3), channel_id=1, source_target_pairs={{480,0},{0,32},{32,64},{64,96},{96,128},{128,160},{160,192},{192,2... | collective-permute-start | bytes 786440 | tf_op jit(solution)/shard_map/while/body/eval_jaxpr/ppermute | solution.py:12
  480.0 20.0 %collective-permute-start = (bf16[2,2,128,1,128]{4,2,0,3,1:T(8,128)(2,1)S(1)}, bf16[2,2,128,1,128]{4,2,0,3,1:T(8,128)(2,1)S(1)}, u32[]{:S(2)}, u32[]{:S(2)}) collective-permute-start(bf16[2,2,128,1,128]{4,2,0,3,1:T(8,128)(2,1)S(1)} %copy.37), channel_id=1, source_target_pairs={{480,0},{0,32},{32,64},{64,96},{96,128},{128,160},{160,192},{192,2... | collective-permute-start | bytes 393224 | tf_op jit(solution)/shard_map/while/body/eval_jaxpr/ppermute | solution.py:12
  512.0 24.2 %collective-permute-start.1 = (f32[2,2,128,1,128]{4,2,0,3,1:T(8,128)S(1)}, f32[2,2,128,1,128]{4,2,0,3,1:T(8,128)S(1)}, u32[]{:S(2)}, u32[]{:S(2)}) collective-permute-start(f32[2,2,128,1,128]{4,2,0,3,1:T(8,128)S(1)} %maximum_add_fusion.3), channel_id=1, source_target_pairs={{480,0},{0,32},{32,64},{64,96},{96,128},{128,160},{160,192},{192,2... | collective-permute-start | bytes 786440 | tf_op jit(solution)/shard_map/while/body/eval_jaxpr/ppermute | solution.py:12
  513.9 22.3 %collective-permute-start = (bf16[2,2,128,1,128]{4,2,0,3,1:T(8,128)(2,1)S(1)}, bf16[2,2,128,1,128]{4,2,0,3,1:T(8,128)(2,1)S(1)}, u32[]{:S(2)}, u32[]{:S(2)}) collective-permute-start(bf16[2,2,128,1,128]{4,2,0,3,1:T(8,128)(2,1)S(1)} %copy.37), channel_id=1, source_target_pairs={{480,0},{0,32},{32,64},{64,96},{96,128},{128,160},{160,192},{192,2... | collective-permute-start | bytes 393224 | tf_op jit(solution)/shard_map/while/body/eval_jaxpr/ppermute | solution.py:12
  537.3 14.5 %collective-permute-start.3 = (f32[2,2,128,1,128]{4,2,0,3,1:T(8,128)S(1)}, f32[2,2,128,1,128]{4,2,0,3,1:T(8,128)S(1)}, u32[]{:S(2)}, u32[]{:S(2)}) collective-permute-start(f32[2,2,128,1,128]{4,2,0,3,1:T(8,128)S(1)} %maximum_add_fusion.1), channel_id=1, source_target_pairs={{480,0},{0,32},{32,64},{64,96},{96,128},{128,160},{160,192},{192,2... | collective-permute-start | bytes 786440 | tf_op jit(solution)/shard_map/ppermute | solution.py:12
  551.8 8.1 %collective-permute-start.4 = (f32[2,128,1,128]{3,1,0,2:T(8,128)S(1)}, f32[2,128,1,128]{3,1,0,2:T(8,128)S(1)}, u32[]{:S(2)}, u32[]{:S(2)}) collective-permute-start(f32[2,128,1,128]{3,1,0,2:T(8,128)S(1)} %slice_bitcast_fusion), channel_id=1, source_target_pairs={{4,0},{8,4},{12,8},{16,12},{20,16},{24,20},{28,24},{5,1},{9,5},{13... | collective-permute-start | bytes 393224 | tf_op jit(solution)/shard_map/ppermute | solution.py:18
where the time goes:
time: 564 us; the launch traced here: 560 us
  waiting for transfers between devices  261 us (46%)
  other arithmetic  173 us (31%)
  starting transfers between devices  85.8 us (15%)
  matrix products  23.2 us (4%)
  local copies, waits for them, and re-layouts  15.1 us (3%)
    ppermute x31, waiting for transfers between devices, from_behind(): return lax.ppermute(block, axis, route)  256 us
    select_n x17, other arithmetic, segment_positions(): return jnp.where(local_rows < span_rows, first_half, second_half)  169 us
    ppermute x31, starting transfers between devices, from_behind(): return lax.ppermute(block, axis, route)  78.3 us
    gather x16, local copies, waits for them, and re-layouts, segment_positions(): rank_value = jnp.take(pair_order, slot_index)  11.6 us
  transfers between devices with their start and end apart: 33, of which 17 were waited for; matrix products, arithmetic and copies ran while one was open for 5% of the time, Pallas kernels for 0%

commit v1 on v0

v1 whole, which is shorter than its diff:
```python
import functools
import math

import jax
import jax.numpy as jnp
from jax import lax
from jax.experimental import pallas as pl
from jax.experimental.pallas import tpu as pltpu
from jax.sharding import PartitionSpec as P

MESH = pl.DeviceIdType.MESH
LOG2E = math.log2(math.e)
X_DEVICES = 4
Y_DEVICES = 4
ROWS = 128
HEADS = 6
DIM = 128
SPAN = 64
GROUP_KEYS = Y_DEVICES * ROWS
PAIRS = HEADS // 2
OUTER = 8

NT = (((1,), (1,)), ((), ()))
TN = (((0,), (0,)), ((), ()))
NN = (((1,), (0,)), ((), ()))


def dot(a, b, dims):
    return lax.dot_general(a, b, dims, preferred_element_type=jnp.float32)


def kernel(
    order_ref, q_ref, k_ref, v_ref, o_ref, g_ref, lse_ref,
    dq_ref, dk_ref, dv_ref,
    kv, qs, gs, stat, kpos, weights, scores, dq_acc, acc,
    sx, rx, sy, ry, sq, rq,
    local_sem, z_send, z_recv, ag_send_y, ag_send_x, ag_recv,
    rs_send_x, rs_recv_x, rs_send_y, rs_recv_y, dq_send, dq_recv,
):
    inner = lax.axis_index("inner")
    outer = lax.axis_index("outer")
    head = lax.axis_index("head")
    x = inner // Y_DEVICES
    y = lax.rem(inner, Y_DEVICES)
    inv_root = 1.0 / math.sqrt(DIM)

    def at_x(distance):
        return (lax.rem(x + distance, X_DEVICES) * Y_DEVICES + y, outer, head)

    def at_y(distance):
        return (x * Y_DEVICES + lax.rem(y + distance, Y_DEVICES), outer, head)

    def at_z(distance):
        return (inner, outer + distance, head)

    def block(xi, yi):
        return kv.at[xi, :, pl.ds(pl.multiple_of(yi * ROWS, ROWS), ROWS), :]

    mine = pl.ds(pl.multiple_of(y * ROWS, ROWS), ROWS)
    loads = [
        pltpu.make_async_copy(k_ref, kv.at[x, 0, mine, :], local_sem.at[0]),
        pltpu.make_async_copy(v_ref, kv.at[x, 1, mine, :], local_sem.at[1]),
        pltpu.make_async_copy(q_ref, qs.at[0], local_sem.at[2]),
        pltpu.make_async_copy(g_ref, gs.at[0], local_sem.at[3]),
    ]
    for load in loads:
        load.start()

    barrier = pltpu.get_barrier_semaphore()
    for distance in (1, 2, 3):
        pl.semaphore_signal(barrier, inc=1, device_id=at_x(distance), device_id_type=MESH)
        pl.semaphore_signal(barrier, inc=1, device_id=at_y(distance), device_id_type=MESH)

    @pl.when(outer > 0)
    def _():
        pl.semaphore_signal(barrier, inc=1, device_id=at_z(-1), device_id_type=MESH)

    @pl.when(outer < OUTER - 1)
    def _():
        pl.semaphore_signal(barrier, inc=1, device_id=at_z(1), device_id_type=MESH)

    for load in loads:
        load.wait()

    stat[0, 0, 0:HEADS, :] = lse_ref[...] * LOG2E
    ones = jnp.ones((8, DIM), jnp.bfloat16)
    for h in range(HEADS):
        product = gs[0, h].astype(jnp.float32) * o_ref[h].astype(jnp.float32)
        high = product.astype(jnp.bfloat16)
        low = (product - high.astype(jnp.float32)).astype(jnp.bfloat16)
        sums = dot(ones, high, NT) + dot(ones, low, NT)
        stat[0, 1, h : h + 1, :] = sums[0:1, :]

    peers = 6 + jnp.minimum(outer, 1) + jnp.minimum(OUTER - 1 - outer, 1)
    pl.semaphore_wait(barrier, peers)

    def send_y(distance):
        return pltpu.make_async_remote_copy(
            block(x, y), block(x, y), ag_send_y.at[distance - 1],
            ag_recv.at[x * Y_DEVICES + y], device_id=at_y(distance), device_id_type=MESH,
        )

    def send_x(step, distance):
        yi = lax.rem(y + step, Y_DEVICES)
        return pltpu.make_async_remote_copy(
            block(x, yi), block(x, yi), ag_send_x.at[step, distance - 1],
            ag_recv.at[x * Y_DEVICES + yi], device_id=at_x(distance), device_id_type=MESH,
        )

    def wait_block(xi, yi):
        pltpu.make_async_remote_copy(
            block(xi, yi), block(xi, yi), ag_send_y.at[0],
            ag_recv.at[xi * Y_DEVICES + yi], device_id=at_y(1), device_id_type=MESH,
        ).wait_recv()

    def z_copies():
        return [
            pltpu.make_async_remote_copy(
                ref.at[0], ref.at[1], z_send.at[i], z_recv.at[i],
                device_id=at_z(-1), device_id_type=MESH,
            )
            for i, ref in enumerate((stat, qs, gs))
        ]

    for distance in (1, 3, 2):
        send_y(distance).start()

    @pl.when(outer > 0)
    def _():
        for copy in z_copies():
            copy.start()

    for distance in (1, 3, 2):
        send_x(0, distance).start()

    row = lax.broadcasted_iota(jnp.int32, (SPAN, DIM), 0)
    for device in range(X_DEVICES * Y_DEVICES):
        rank = order_ref[device]
        xi, yi = divmod(device, Y_DEVICES)
        kpos[xi, yi * ROWS : yi * ROWS + SPAN, :] = row + rank * SPAN
        kpos[xi, yi * ROWS + SPAN : (yi + 1) * ROWS, :] = (
            row + (2 * X_DEVICES * Y_DEVICES - 1 - rank) * SPAN
        )
    lane = lax.broadcasted_iota(jnp.int32, (1, ROWS), 1)
    rank = order_ref[inner]
    qpos = jnp.where(
        lane < SPAN,
        rank * SPAN + lane,
        (2 * X_DEVICES * Y_DEVICES - 1 - rank) * SPAN + lane - SPAN,
    )
    qpos = jnp.concatenate([qpos, qpos], axis=1)

    dq_acc[...] = jnp.zeros_like(dq_acc)

    for step in (1, 3, 2):
        wait_block(x, lax.rem(y + step, Y_DEVICES))
        for distance in (1, 3, 2):
            send_x(step, distance).start()

    def tile(xi, half, masked):
        keys = kv[xi, 0]
        values = kv[xi, 1]
        if masked:
            column = kpos[xi]
            column = jnp.concatenate([column, column], axis=1)
        for pair in range(PAIRS):
            two = slice(2 * pair, 2 * pair + 2)
            q_two = qs[half, two].reshape(2 * ROWS, DIM)
            g_two = gs[half, two].reshape(2 * ROWS, DIM)
            norms = jnp.concatenate(
                [stat[half, 0, 2 * pair + i : 2 * pair + i + 1, :] for i in (0, 1)], axis=1
            )
            dots = jnp.concatenate(
                [stat[half, 1, 2 * pair + i : 2 * pair + i + 1, :] for i in (0, 1)], axis=1
            )
            p = jnp.exp2(dot(keys, q_two, NT) * (inv_root * LOG2E) - norms)
            if masked:
                p = jnp.where(column <= qpos, p, 0.0)
            lanes = slice(2 * pair * ROWS, 2 * (pair + 1) * ROWS)
            weights[:, lanes] = p.astype(jnp.bfloat16)
            ds = (p * (dot(values, g_two, NT) - dots)).astype(jnp.bfloat16)
            scores[:, lanes] = ds
            dq_acc[half, lanes, :] += dot(ds, keys, TN)
        grad_k = dot(scores[...], qs[half].reshape(HEADS * ROWS, DIM), NN)
        grad_v = dot(weights[...], gs[half].reshape(HEADS * ROWS, DIM), NN)
        return grad_k, grad_v

    def own_tile(distance):
        xi = lax.rem(x + distance, X_DEVICES)
        grad_k, grad_v = tile(xi, 0, True)
        acc[xi, 0] = grad_k
        acc[xi, 1] = grad_v

    def wait_group(distance):
        xi = lax.rem(x + distance, X_DEVICES)
        for yi in range(Y_DEVICES):
            wait_block(xi, lax.rem(y + yi, Y_DEVICES))

    own_tile(0)
    for distance in (1, 3, 2):
        wait_group(distance)
        own_tile(distance)

    @pl.when(outer < OUTER - 1)
    def _():
        for copy in z_copies():
            copy.wait_recv()

    @pl.when(outer == OUTER - 1)
    def _():
        stat[1] = jnp.zeros_like(stat[1])
        qs[1] = jnp.zeros_like(qs[1])
        gs[1] = jnp.zeros_like(gs[1])

    def next_tile(distance):
        xi = lax.rem(x + distance, X_DEVICES)
        grad_k, grad_v = tile(xi, 1, False)
        return (acc[xi, 0] + grad_k) * inv_root, acc[xi, 1] + grad_v

    def rs_x(distance):
        return pltpu.make_async_remote_copy(
            sx.at[distance - 1], rx.at[distance - 1], rs_send_x.at[distance - 1],
            rs_recv_x.at[distance - 1], device_id=at_x(distance), device_id_type=MESH,
        )

    for distance in (2, 1, 3):
        grad_k, grad_v = next_tile(distance)
        sx[distance - 1, 0] = grad_k.astype(jnp.bfloat16)
        sx[distance - 1, 1] = grad_v.astype(jnp.bfloat16)
        rs_x(distance).start()
    grad_k, grad_v = next_tile(0)
    acc[x, 0] = grad_k
    acc[x, 1] = grad_v

    def dq_copy():
        return pltpu.make_async_remote_copy(
            sq, rq, dq_send, dq_recv, device_id=at_z(1), device_id_type=MESH
        )

    @pl.when(outer < OUTER - 1)
    def _():
        sq[...] = (dq_acc[1] * inv_root).astype(jnp.bfloat16)
        dq_copy().start()

    for distance in (1, 2, 3):
        rs_x(distance).wait_recv()

    def rs_y(distance):
        return pltpu.make_async_remote_copy(
            sy.at[distance - 1], ry.at[distance - 1], rs_send_y.at[distance - 1],
            rs_recv_y.at[distance - 1], device_id=at_y(distance), device_id_type=MESH,
        )

    def over_x(distance):
        yi = lax.rem(y + distance, Y_DEVICES)
        rows = pl.ds(pl.multiple_of(yi * ROWS, ROWS), ROWS)
        total = acc[x, :, rows, :]
        for i in range(X_DEVICES - 1):
            total = total + rx[i, :, rows, :].astype(jnp.float32)
        return total

    for distance in (2, 1, 3):
        sy[distance - 1] = over_x(distance).astype(jnp.bfloat16)
        rs_y(distance).start()
    total = over_x(0)

    @pl.when(outer > 0)
    def _():
        pltpu.make_async_remote_copy(
            sq, rq, dq_send, dq_recv, device_id=at_z(-1), device_id_type=MESH
        ).wait_recv()

    @pl.when(outer == 0)
    def _():
        rq[...] = jnp.zeros_like(rq)

    dq_ref[...] = (
        (dq_acc[0] * inv_root + rq[...].astype(jnp.float32))
        .astype(jnp.bfloat16)
        .reshape(HEADS, ROWS, DIM)
    )

    for distance in (1, 2, 3):
        rs_y(distance).wait_recv()
        total = total + ry[distance - 1].astype(jnp.float32)
    dk_ref[...] = total[0].astype(jnp.bfloat16)
    dv_ref[...] = total[1].astype(jnp.bfloat16)

    for distance in (1, 2, 3):
        send_y(distance).wait_send()
        rs_x(distance).wait_send()
        rs_y(distance).wait_send()
        for step in range(Y_DEVICES):
            send_x(step, distance).wait_send()

    @pl.when(outer > 0)
    def _():
        for copy in z_copies():
            copy.wait_send()

    @pl.when(outer < OUTER - 1)
    def _():
        dq_copy().wait_send()


def on_device(queries, key_rows, value_rows, attn_out, grad_out, log_norms, pair_order):
    def heads_first(rows):
        return jnp.transpose(rows, (1, 0, 2))

    half = jnp.bfloat16
    full = jnp.float32
    dma = pltpu.SemaphoreType.DMA
    vmem = pl.BlockSpec(memory_space=pltpu.VMEM)
    hbm = pl.BlockSpec(memory_space=pl.ANY)
    grad_queries, grad_keys, grad_values = pl.pallas_call(
        kernel,
        out_shape=(
            jax.ShapeDtypeStruct((HEADS, ROWS, DIM), half),
            jax.ShapeDtypeStruct((ROWS, DIM), half),
            jax.ShapeDtypeStruct((ROWS, DIM), half),
        ),
        in_specs=[
            pl.BlockSpec(memory_space=pltpu.SMEM), hbm, hbm, hbm, vmem, hbm, vmem,
        ],
        out_specs=(vmem, vmem, vmem),
        scratch_shapes=[
            pltpu.VMEM((X_DEVICES, 2, GROUP_KEYS, DIM), half),
            pltpu.VMEM((2, HEADS, ROWS, DIM), half),
            pltpu.VMEM((2, HEADS, ROWS, DIM), half),
            pltpu.VMEM((2, 2, 8, ROWS), full),
            pltpu.VMEM((X_DEVICES, GROUP_KEYS, DIM), jnp.int32),
            pltpu.VMEM((GROUP_KEYS, HEADS * ROWS), half),
            pltpu.VMEM((GROUP_KEYS, HEADS * ROWS), half),
            pltpu.VMEM((2, HEADS * ROWS, DIM), full),
            pltpu.VMEM((X_DEVICES, 2, GROUP_KEYS, DIM), full),
            pltpu.VMEM((3, 2, GROUP_KEYS, DIM), half),
            pltpu.VMEM((3, 2, GROUP_KEYS, DIM), half),
            pltpu.VMEM((3, 2, ROWS, DIM), half),
            pltpu.VMEM((3, 2, ROWS, DIM), half),
            pltpu.VMEM((HEADS * ROWS, DIM), half),
            pltpu.VMEM((HEADS * ROWS, DIM), half),
            dma((4,)), dma((3,)), dma((3,)), dma((3,)), dma((4, 3)), dma((16,)),
            dma((3,)), dma((3,)), dma((3,)), dma((3,)), dma, dma,
        ],
        compiler_params=pltpu.CompilerParams(
            collective_id=0, has_side_effects=True, vmem_limit_bytes=60 * 2**20
        ),
        cost_estimate=pl.CostEstimate(
            flops=4 * 10**9, bytes_accessed=10**6, transcendentals=3 * 10**6
        ),
    )(
        pair_order,
        heads_first(queries),
        key_rows.reshape(ROWS, DIM),
        value_rows.reshape(ROWS, DIM),
        heads_first(attn_out),
        heads_first(grad_out),
        log_norms,
    )
    return (
        jnp.transpose(grad_queries, (1, 0, 2)),
        grad_keys.reshape(ROWS, 1, DIM),
        grad_values.reshape(ROWS, 1, DIM),
    )


def solution(mesh):
    rows = P(("outer", "inner"), "head", None)
    return jax.shard_map(
        on_device,
        mesh=mesh,
        in_specs=(rows, rows, rows, rows, rows, P("head", ("outer", "inner")), P()),
        out_specs=(rows, rows, rows),
        check_vma=False,
    )
```

time: 564 us -> 55.3 us (0.10)
  the two profiles are of different devices: /device:TPU:204 before, /device:TPU:2 now
where the time goes in v1:
time: 55.3 us; the launch traced here: 55 us
  Pallas kernels  51.4 us (93%)
  local copies, waits for them, and re-layouts  3.01 us (5%)
  between operations  0.65 us (1%)
    pallas_call x1, Pallas kernels, on_device(): pl.pallas_call(kernel, out_shape=(jax.ShapeDtypeStruct((HEADS, ROWS, DIM)...  51.4 us
    unnamed x7, local copies, waits for them, and re-layouts  3.01 us

profile of v1, /device:TPU:2, one launch (start us, length us, event | category | flops | bytes accessed | tf_op | source)
XLA Modules:
  0.0 55.0 jit_solution(1214326943703755661)
XLA Ops:
  0.6 51.4 %shard_map.94 = (bf16[6,128,128]{2,1,0:T(8,128)(2,1)}, bf16[128,128]{1,0:T(8,128)(2,1)}, bf16[128,128]{1,0:T(8,128)(2,1)}) custom-call(s32[16]{0:T(128)} %order_ref.1, bf16[6,128,128]{2,1,0:T(8,128)(2,1)} %bitcast.11, bf16[128,128]{1,0:T(8,128)(2,1)} %bitcast.14, bf16[128,128]{1,0:T(8,128)(2,1)} %bitcast.15, bf16[6,128,128]{2,1,0:T(8,128)(2,1)} %bitcast.12, ...), custom_call_target="tpu_custom_call" | custom-call | flops 4000000000 | bytes 1000000 | tf_op jit(solution)/shard_map/pallas_call | solution.py:315
  52.0 0.0 copy-start.1
  52.0 1.6 %copy.13 = bf16[128,6,128]{2,0,1:T(8,128)(2,1)} copy(bf16[128,6,128]{2,0,1:T(8,128)(2,1)} %bitcast.8) | data formatting | bytes 393216
  53.7 0.0 copy-done.1
  53.7 0.0 copy-start
  53.7 0.6 %copy.14 = bf16[128,1,128]{2,0,1:T(8,128)(2,1)} copy(bf16[128,1,128]{2,0,1:T(8,128)(2,1)S(1)} %bitcast.10) | data formatting | bytes 65536
  54.3 0.2 copy-done
  54.4 0.6 %copy.15 = bf16[128,1,128]{2,0,1:T(8,128)(2,1)} copy(bf16[128,1,128]{2,0,1:T(8,128)(2,1)S(1)} %bitcast.9) | data formatting | bytes 65536
Async XLA Ops:
  52.0 1.6 %copy-start.1 = (bf16[128,128]{1,0:T(8,128)(2,1)S(1)}, bf16[128,128]{1,0:T(8,128)(2,1)}, u32[]{:S(2)}) copy-start(bf16[128,128]{1,0:T(8,128)(2,1)} %get-tuple-element.7) | copy-start | bytes 98308
  53.7 0.8 %copy-start = (bf16[128,128]{1,0:T(8,128)(2,1)S(1)}, bf16[128,128]{1,0:T(8,128)(2,1)}, u32[]{:S(2)}) copy-start(bf16[128,128]{1,0:T(8,128)(2,1)} %get-tuple-element.8) | copy-start | bytes 98308

commit v2 on v1

v2 whole, which is shorter than its diff:
```python
import functools
import math

import jax
import jax.numpy as jnp
from jax import lax
from jax.experimental import pallas as pl
from jax.experimental.pallas import tpu as pltpu
from jax.sharding import PartitionSpec as P

MESH = pl.DeviceIdType.MESH
LOG2E = math.log2(math.e)
X_DEVICES = 4
Y_DEVICES = 4
ROWS = 128
HEADS = 6
DIM = 128
SPAN = 64
GROUP_KEYS = Y_DEVICES * ROWS
PAIRS = HEADS // 2
OUTER = 8

NT = (((1,), (1,)), ((), ()))
TN = (((0,), (0,)), ((), ()))
NN = (((1,), (0,)), ((), ()))


def dot(a, b, dims):
    return lax.dot_general(a, b, dims, preferred_element_type=jnp.float32)


def kernel(
    order_ref, q_ref, k_ref, v_ref, o_ref, g_ref, lse_ref,
    dq_ref, dk_ref, dv_ref,
    kv, qs, gs, attn, lse, stat, kpos, weights, own_scores, next_scores, acc,
    sx, rx, sy, ry, sq, rq,
    local_sem, z_send, z_recv, ag_send_y, ag_send_x, ag_recv,
    rs_send_x, rs_recv_x, rs_send_y, rs_recv_y, dq_send, dq_recv,
):
    inner = lax.axis_index("inner")
    outer = lax.axis_index("outer")
    head = lax.axis_index("head")
    x = inner // Y_DEVICES
    y = lax.rem(inner, Y_DEVICES)
    inv_root = 1.0 / math.sqrt(DIM)

    def at_x(distance):
        return (lax.rem(x + distance, X_DEVICES) * Y_DEVICES + y, outer, head)

    def at_y(distance):
        return (x * Y_DEVICES + lax.rem(y + distance, Y_DEVICES), outer, head)

    def at_z(distance):
        return (inner, outer + distance, head)

    def rows_of(xi):
        return pl.ds(pl.multiple_of(xi * ROWS, ROWS), ROWS)

    def block(xi, yi):
        return kv.at[yi, :, rows_of(xi), :]

    loads = [
        pltpu.make_async_copy(k_ref, kv.at[y, 0, rows_of(x), :], local_sem.at[0]),
        pltpu.make_async_copy(v_ref, kv.at[y, 1, rows_of(x), :], local_sem.at[1]),
        pltpu.make_async_copy(g_ref, gs.at[0], local_sem.at[2]),
        pltpu.make_async_copy(o_ref, attn, local_sem.at[3]),
        pltpu.make_async_copy(lse_ref, lse, local_sem.at[4]),
        pltpu.make_async_copy(q_ref, qs.at[0], local_sem.at[5]),
    ]
    for load in loads:
        load.start()

    barrier = pltpu.get_barrier_semaphore()
    for distance in (1, 2, 3):
        pl.semaphore_signal(barrier, inc=1, device_id=at_x(distance), device_id_type=MESH)
        pl.semaphore_signal(barrier, inc=1, device_id=at_y(distance), device_id_type=MESH)

    @pl.when(outer > 0)
    def _():
        pl.semaphore_signal(barrier, inc=1, device_id=at_z(-1), device_id_type=MESH)

    @pl.when(outer < OUTER - 1)
    def _():
        pl.semaphore_signal(barrier, inc=1, device_id=at_z(1), device_id_type=MESH)

    for load in loads:
        load.wait()

    stat[0, 0, 0:HEADS, :] = lse[...] * LOG2E
    ones = jnp.ones((8, DIM), jnp.bfloat16)
    for h in range(HEADS):
        product = gs[0, h].astype(jnp.float32) * attn[h].astype(jnp.float32)
        high = product.astype(jnp.bfloat16)
        low = (product - high.astype(jnp.float32)).astype(jnp.bfloat16)
        sums = dot(ones, high, NT) + dot(ones, low, NT)
        stat[0, 1, h : h + 1, :] = sums[0:1, :]

    row = lax.broadcasted_iota(jnp.int32, (SPAN, DIM), 0)
    for device in range(X_DEVICES * Y_DEVICES):
        rank = order_ref[device]
        xi, yi = divmod(device, Y_DEVICES)
        kpos[yi, xi * ROWS : xi * ROWS + SPAN, :] = row + rank * SPAN
        kpos[yi, xi * ROWS + SPAN : (xi + 1) * ROWS, :] = (
            row + (2 * X_DEVICES * Y_DEVICES - 1 - rank) * SPAN
        )
    lane = lax.broadcasted_iota(jnp.int32, (1, ROWS), 1)
    rank = order_ref[inner]
    qpos = jnp.where(
        lane < SPAN,
        rank * SPAN + lane,
        (2 * X_DEVICES * Y_DEVICES - 1 - rank) * SPAN + lane - SPAN,
    )
    qpos = jnp.concatenate([qpos, qpos], axis=1)

    peers = 6 + jnp.minimum(outer, 1) + jnp.minimum(OUTER - 1 - outer, 1)
    pl.semaphore_wait(barrier, peers)

    def send_y(distance):
        return pltpu.make_async_remote_copy(
            block(x, y), block(x, y), ag_send_y.at[distance - 1],
            ag_recv.at[x * Y_DEVICES + y], device_id=at_y(distance), device_id_type=MESH,
        )

    def send_x(step, distance):
        yi = lax.rem(y + step, Y_DEVICES)
        return pltpu.make_async_remote_copy(
            block(x, yi), block(x, yi), ag_send_x.at[step, distance - 1],
            ag_recv.at[x * Y_DEVICES + yi], device_id=at_x(distance), device_id_type=MESH,
        )

    def wait_block(xi, yi):
        pltpu.make_async_remote_copy(
            block(xi, yi), block(xi, yi), ag_send_y.at[0],
            ag_recv.at[xi * Y_DEVICES + yi], device_id=at_y(1), device_id_type=MESH,
        ).wait_recv()

    def z_copies():
        return [
            pltpu.make_async_remote_copy(
                ref.at[0], ref.at[1], z_send.at[i], z_recv.at[i],
                device_id=at_z(-1), device_id_type=MESH,
            )
            for i, ref in enumerate((stat, qs, gs))
        ]

    for distance in (1, 3, 2):
        send_y(distance).start()

    for distance in (1, 3, 2):
        send_x(0, distance).start()

    @pl.when(outer > 0)
    def _():
        for copy in z_copies():
            copy.start()

    def tile(step, half, scores):
        yi = lax.rem(y + step, Y_DEVICES)
        keys = kv[yi, 0]
        values = kv[yi, 1]
        if half == 0:
            column = kpos[yi]
            column = jnp.concatenate([column, column], axis=1)
        for pair in range(PAIRS):
            two = slice(2 * pair, 2 * pair + 2)
            q_two = qs[half, two].reshape(2 * ROWS, DIM)
            g_two = gs[half, two].reshape(2 * ROWS, DIM)
            norms = jnp.concatenate(
                [stat[half, 0, 2 * pair + i : 2 * pair + i + 1, :] for i in (0, 1)], axis=1
            )
            dots = jnp.concatenate(
                [stat[half, 1, 2 * pair + i : 2 * pair + i + 1, :] for i in (0, 1)], axis=1
            )
            p = jnp.exp2(dot(keys, q_two, NT) * (inv_root * LOG2E) - norms)
            if half == 0:
                p = jnp.where(column <= qpos, p, 0.0)
            lanes = slice(2 * pair * ROWS, 2 * (pair + 1) * ROWS)
            weights[:, lanes] = p.astype(jnp.bfloat16)
            ds = (p * (dot(values, g_two, NT) - dots)).astype(jnp.bfloat16)
            scores[step, :, lanes] = ds
        grad_k = dot(scores[step], qs[half].reshape(HEADS * ROWS, DIM), NN)
        grad_v = dot(weights[...], gs[half].reshape(HEADS * ROWS, DIM), NN)
        return grad_k, grad_v

    def own_tile(step):
        grad_k, grad_v = tile(step, 0, own_scores)
        acc[step, 0] = grad_k
        acc[step, 1] = grad_v

    def query_grads(scores):
        total = jnp.zeros((HEADS * ROWS, DIM), jnp.float32)
        for step in range(Y_DEVICES):
            total = total + dot(scores[step], kv[lax.rem(y + step, Y_DEVICES), 0], TN)
        return total * inv_root

    def pass_on(step):
        wait_block(x, lax.rem(y + step, Y_DEVICES))
        for distance in (1, 3, 2):
            send_x(step, distance).start()

    def wait_others(step):
        for distance in (1, 3, 2):
            wait_block(lax.rem(x + distance, X_DEVICES), lax.rem(y + step, Y_DEVICES))

    pass_on(1)
    pass_on(3)
    wait_others(0)
    own_tile(0)
    pass_on(2)
    for step in (1, 3, 2):
        wait_others(step)
        own_tile(step)

    @pl.when(outer < OUTER - 1)
    def _():
        for copy in z_copies():
            copy.wait_recv()

    @pl.when(outer == OUTER - 1)
    def _():
        stat[1] = jnp.zeros_like(stat[1])
        qs[1] = jnp.zeros_like(qs[1])
        gs[1] = jnp.zeros_like(gs[1])

    def rs_x(step, distance):
        xi = lax.rem(x + distance, X_DEVICES)
        return pltpu.make_async_remote_copy(
            sx.at[step, :, rows_of(xi), :], rx.at[step, distance - 1],
            rs_send_x.at[step, distance - 1], rs_recv_x.at[step, distance - 1],
            device_id=at_x(distance), device_id_type=MESH,
        )

    def rs_y(step):
        return pltpu.make_async_remote_copy(
            sy.at[step - 1], ry.at[step - 1], rs_send_y.at[step - 1],
            rs_recv_y.at[step - 1], device_id=at_y(step), device_id_type=MESH,
        )

    def next_tile(step):
        grad_k, grad_v = tile(step, 1, next_scores)
        grad_k = (acc[step, 0] + grad_k) * inv_root
        grad_v = acc[step, 1] + grad_v
        acc[step, 0] = grad_k
        acc[step, 1] = grad_v
        sx[step, 0] = grad_k.astype(jnp.bfloat16)
        sx[step, 1] = grad_v.astype(jnp.bfloat16)
        for distance in (2, 1, 3):
            rs_x(step, distance).start()

    def over_x(step):
        total = acc[step, :, rows_of(x), :]
        for distance in (1, 2, 3):
            rs_x(step, distance).wait_recv()
            total = total + rx[step, distance - 1].astype(jnp.float32)
        return total

    def to_y(step):
        sy[step - 1] = over_x(step).astype(jnp.bfloat16)
        rs_y(step).start()

    next_tile(2)
    next_tile(1)
    next_tile(3)
    to_y(2)
    next_tile(0)
    to_y(1)

    def dq_copy(distance):
        return pltpu.make_async_remote_copy(
            sq, rq, dq_send, dq_recv, device_id=at_z(distance), device_id_type=MESH
        )

    sq[...] = query_grads(next_scores).astype(jnp.bfloat16)

    @pl.when(outer < OUTER - 1)
    def _():
        dq_copy(1).start()

    to_y(3)
    total = over_x(0)
    own = query_grads(own_scores)

    @pl.when(outer > 0)
    def _():
        dq_copy(-1).wait_recv()

    @pl.when(outer == 0)
    def _():
        rq[...] = jnp.zeros_like(rq)

    dq_ref[...] = (
        (own + rq[...].astype(jnp.float32)).astype(jnp.bfloat16).reshape(HEADS, ROWS, DIM)
    )

    for step in (1, 2, 3):
        rs_y(step).wait_recv()
        total = total + ry[step - 1].astype(jnp.float32)
    dk_ref[...] = total[0].astype(jnp.bfloat16)
    dv_ref[...] = total[1].astype(jnp.bfloat16)

    for distance in (1, 2, 3):
        send_y(distance).wait_send()
        rs_y(distance).wait_send()
        for step in range(Y_DEVICES):
            send_x(step, distance).wait_send()
            rs_x(step, distance).wait_send()

    @pl.when(outer > 0)
    def _():
        for copy in z_copies():
            copy.wait_send()

    @pl.when(outer < OUTER - 1)
    def _():
        dq_copy(1).wait_send()


def store_kernel(dq_in, dk_in, dv_in, dq_ref, dk_ref, dv_ref, sems):
    copies = [
        pltpu.make_async_copy(dq_in, dq_ref, sems.at[0]),
        pltpu.make_async_copy(dk_in, dk_ref, sems.at[1]),
        pltpu.make_async_copy(dv_in, dv_ref, sems.at[2]),
    ]
    for copy in copies:
        copy.start()
    for copy in copies:
        copy.wait()


def on_device(queries, key_rows, value_rows, attn_out, grad_out, log_norms, pair_order):
    def heads_first(rows):
        return jnp.transpose(rows, (1, 0, 2))

    half = jnp.bfloat16
    full = jnp.float32
    dma = pltpu.SemaphoreType.DMA
    vmem = pl.BlockSpec(memory_space=pltpu.VMEM)
    hbm = pl.BlockSpec(memory_space=pltpu.HBM)
    grads = (
        jax.ShapeDtypeStruct((HEADS, ROWS, DIM), half),
        jax.ShapeDtypeStruct((ROWS, DIM), half),
        jax.ShapeDtypeStruct((ROWS, DIM), half),
    )
    parts = pl.pallas_call(
        kernel,
        out_shape=grads,
        in_specs=[pl.BlockSpec(memory_space=pltpu.SMEM), hbm, hbm, hbm, hbm, hbm, hbm],
        out_specs=(vmem, vmem, vmem),
        scratch_shapes=[
            pltpu.VMEM((Y_DEVICES, 2, GROUP_KEYS, DIM), half),
            pltpu.VMEM((2, HEADS, ROWS, DIM), half),
            pltpu.VMEM((2, HEADS, ROWS, DIM), half),
            pltpu.VMEM((HEADS, ROWS, DIM), half),
            pltpu.VMEM((HEADS, ROWS), full),
            pltpu.VMEM((2, 2, 8, ROWS), full),
            pltpu.VMEM((Y_DEVICES, GROUP_KEYS, DIM), jnp.int32),
            pltpu.VMEM((GROUP_KEYS, HEADS * ROWS), half),
            pltpu.VMEM((Y_DEVICES, GROUP_KEYS, HEADS * ROWS), half),
            pltpu.VMEM((Y_DEVICES, GROUP_KEYS, HEADS * ROWS), half),
            pltpu.VMEM((Y_DEVICES, 2, GROUP_KEYS, DIM), full),
            pltpu.VMEM((Y_DEVICES, 2, GROUP_KEYS, DIM), half),
            pltpu.VMEM((Y_DEVICES, 3, 2, ROWS, DIM), half),
            pltpu.VMEM((3, 2, ROWS, DIM), half),
            pltpu.VMEM((3, 2, ROWS, DIM), half),
            pltpu.VMEM((HEADS * ROWS, DIM), half),
            pltpu.VMEM((HEADS * ROWS, DIM), half),
            dma((6,)), dma((3,)), dma((3,)), dma((3,)), dma((4, 3)), dma((16,)),
            dma((4, 3)), dma((4, 3)), dma((3,)), dma((3,)), dma, dma,
        ],
        compiler_params=pltpu.CompilerParams(
            collective_id=0, has_side_effects=True, vmem_limit_bytes=60 * 2**20
        ),
        cost_estimate=pl.CostEstimate(
            flops=4 * 10**9, bytes_accessed=10**6, transcendentals=3 * 10**6
        ),
    )(
        pair_order,
        heads_first(queries),
        key_rows.reshape(ROWS, DIM),
        value_rows.reshape(ROWS, DIM),
        heads_first(attn_out),
        heads_first(grad_out),
        log_norms,
    )
    grad_queries, grad_keys, grad_values = pl.pallas_call(
        store_kernel,
        out_shape=grads,
        in_specs=[vmem, vmem, vmem],
        out_specs=(hbm, hbm, hbm),
        scratch_shapes=[dma((3,))],
    )(*parts)
    return (
        jnp.transpose(grad_queries, (1, 0, 2)),
        grad_keys.reshape(ROWS, 1, DIM),
        grad_values.reshape(ROWS, 1, DIM),
    )


def solution(mesh):
    rows = P(("outer", "inner"), "head", None)
    return jax.shard_map(
        on_device,
        mesh=mesh,
        in_specs=(rows, rows, rows, rows, rows, P("head", ("outer", "inner")), P()),
        out_specs=(rows, rows, rows),
        check_vma=False,
    )
```

time: 55.3 us -> 45.5 us (0.82)
  the two profiles are of different devices: /device:TPU:2 before, /device:TPU:390 now
where the time goes in v2:
time: 45.5 us; the launch traced here: 45.3 us
  Pallas kernels  44.7 us (98%)
  between operations  0.64 us (1%)
    pallas_call x1, Pallas kernels, on_device(): pl.pallas_call(kernel, out_shape=grads, in_specs=[pl.BlockSpec(memory_spa...  43 us
    pallas_call x1, Pallas kernels, on_device(): pl.pallas_call(store_kernel, out_shape=grads, in_specs=[vmem, vmem, vmem]...  1.67 us

profile of v2, /device:TPU:390, one launch (start us, length us, event | category | flops | bytes accessed | tf_op | source)
XLA Modules:
  0.0 45.3 jit_solution(1017983307774476973)
XLA Ops:
  0.6 43.0 %shard_map.94 = (bf16[6,128,128]{2,1,0:T(8,128)(2,1)}, bf16[128,128]{1,0:T(8,128)(2,1)}, bf16[128,128]{1,0:T(8,128)(2,1)}) custom-call(s32[16]{0:T(128)} %order_ref.1, bf16[6,128,128]{2,1,0:T(8,128)(2,1)} %bitcast.8, bf16[128,128]{1,0:T(8,128)(2,1)} %bitcast.12, bf16[128,128]{1,0:T(8,128)(2,1)} %bitcast.13, bf16[6,128,128]{2,1,0:T(8,128)(2,1)} %bitcast.9, ...), custom_call_target="tpu_custom_call" | custom-call | flops 4000000000 | bytes 1000000 | tf_op jit(solution)/shard_map/pallas_call | solution.py:344
  43.7 1.7 %shard_map.95 = (bf16[6,128,128]{2,1,0:T(8,128)(2,1)}, bf16[128,128]{1,0:T(8,128)(2,1)}, bf16[128,128]{1,0:T(8,128)(2,1)}) custom-call(bf16[6,128,128]{2,1,0:T(8,128)(2,1)} %get-tuple-element.9.dq_in, bf16[128,128]{1,0:T(8,128)(2,1)} %get-tuple-element.10.dk_in, bf16[128,128]{1,0:T(8,128)(2,1)} %get-tuple-element.11.dv_in), custom_call_target="tpu_custom_call" | custom-call | tf_op jit(solution)/shard_map/pallas_call | solution.py:385

commit v3 on v2

--- a/solution.py
+++ b/solution.py
@@ -32,9 +32,9 @@
 def kernel(
     order_ref, q_ref, k_ref, v_ref, o_ref, g_ref, lse_ref,
     dq_ref, dk_ref, dv_ref,
-    kv, qs, gs, attn, lse, stat, kpos, weights, own_scores, next_scores, acc,
-    sx, rx, sy, ry, sq, rq,
-    local_sem, z_send, z_recv, ag_send_y, ag_send_x, ag_recv,
+    kv, qs, gs, attn, lse, stat, kpos, weights, own_scores, next_scores, acc, dq_next,
+    sx, rx, sy, ry, sq, rq, dq_out, dkv_out,
+    local_sem, z_send, z_recv, ag_send_y, ag_send_own, ag_send_x, ag_recv,
     rs_send_x, rs_recv_x, rs_send_y, rs_recv_y, dq_send, dq_recv,
 ):
     inner = lax.axis_index("inner")
@@ -56,8 +56,8 @@
     def rows_of(xi):
         return pl.ds(pl.multiple_of(xi * ROWS, ROWS), ROWS)
 
-    def block(xi, yi):
-        return kv.at[yi, :, rows_of(xi), :]
+    def block(xi, yi, i):
+        return kv.at[yi, i, rows_of(xi), :]
 
     loads = [
         pltpu.make_async_copy(k_ref, kv.at[y, 0, rows_of(x), :], local_sem.at[0]),
@@ -83,6 +83,55 @@
     def _():
         pl.semaphore_signal(barrier, inc=1, device_id=at_z(1), device_id_type=MESH)
 
+    peers = 6 + jnp.minimum(outer, 1) + jnp.minimum(OUTER - 1 - outer, 1)
+    pl.semaphore_wait(barrier, peers)
+
+    def send_own(i, target, sems, slot):
+        return pltpu.make_async_remote_copy(
+            (k_ref, v_ref)[i], block(x, y, i), sems.at[slot, i],
+            ag_recv.at[x * Y_DEVICES + y, i], device_id=target, device_id_type=MESH,
+        )
+
+    def send_y(distance, i):
+        return send_own(i, at_y(distance), ag_send_y, distance - 1)
+
+    def send_x(step, distance, i):
+        if step == 0:
+            return send_own(i, at_x(distance), ag_send_own, distance - 1)
+        yi = lax.rem(y + step, Y_DEVICES)
+        return pltpu.make_async_remote_copy(
+            block(x, yi, i), block(x, yi, i), ag_send_x.at[step - 1, distance - 1, i],
+            ag_recv.at[x * Y_DEVICES + yi, i], device_id=at_x(distance), device_id_type=MESH,
+        )
+
+    def wait_block(xi, yi, i):
+        pltpu.make_async_remote_copy(
+            block(xi, yi, i), block(xi, yi, i), ag_send_y.at[0, 0],
+            ag_recv.at[xi * Y_DEVICES + yi, i], device_id=at_y(1), device_id_type=MESH,
+        ).wait_recv()
+
+    def z_copies():
+        return [
+            pltpu.make_async_remote_copy(
+                source, landing.at[1], z_send.at[i], z_recv.at[i],
+                device_id=at_z(-1), device_id_type=MESH,
+            )
+            for i, (source, landing) in enumerate(((q_ref, qs), (g_ref, gs), (stat.at[0], stat)))
+        ]
+
+    @pl.when(outer > 0)
+    def _():
+        for copy in z_copies()[:2]:
+            copy.start()
+
+    for i in (0, 1):
+        for distance in (1, 3, 2):
+            send_y(distance, i).start()
+
+    for i in (0, 1):
+        for distance in (1, 3, 2):
+            send_x(0, distance, i).start()
+
     for load in loads:
         load.wait()
 
@@ -112,47 +161,9 @@
     )
     qpos = jnp.concatenate([qpos, qpos], axis=1)
 
-    peers = 6 + jnp.minimum(outer, 1) + jnp.minimum(OUTER - 1 - outer, 1)
-    pl.semaphore_wait(barrier, peers)
-
-    def send_y(distance):
-        return pltpu.make_async_remote_copy(
-            block(x, y), block(x, y), ag_send_y.at[distance - 1],
-            ag_recv.at[x * Y_DEVICES + y], device_id=at_y(distance), device_id_type=MESH,
-        )
-
-    def send_x(step, distance):
-        yi = lax.rem(y + step, Y_DEVICES)
-        return pltpu.make_async_remote_copy(
-            block(x, yi), block(x, yi), ag_send_x.at[step, distance - 1],
-            ag_recv.at[x * Y_DEVICES + yi], device_id=at_x(distance), device_id_type=MESH,
-        )
-
-    def wait_block(xi, yi):
-        pltpu.make_async_remote_copy(
-            block(xi, yi), block(xi, yi), ag_send_y.at[0],
-            ag_recv.at[xi * Y_DEVICES + yi], device_id=at_y(1), device_id_type=MESH,
-        ).wait_recv()
-
-    def z_copies():
-        return [
-            pltpu.make_async_remote_copy(
-                ref.at[0], ref.at[1], z_send.at[i], z_recv.at[i],
-                device_id=at_z(-1), device_id_type=MESH,
-            )
-            for i, ref in enumerate((stat, qs, gs))
-        ]
-
-    for distance in (1, 3, 2):
-        send_y(distance).start()
-
-    for distance in (1, 3, 2):
-        send_x(0, distance).start()
-
     @pl.when(outer > 0)
     def _():
-        for copy in z_copies():
-            copy.start()
+        z_copies()[2].start()
 
     def tile(step, half, scores):
         yi = lax.rem(y + step, Y_DEVICES)
@@ -178,38 +189,91 @@
             weights[:, lanes] = p.astype(jnp.bfloat16)
             ds = (p * (dot(values, g_two, NT) - dots)).astype(jnp.bfloat16)
             scores[step, :, lanes] = ds
-        grad_k = dot(scores[step], qs[half].reshape(HEADS * ROWS, DIM), NN)
-        grad_v = dot(weights[...], gs[half].reshape(HEADS * ROWS, DIM), NN)
-        return grad_k, grad_v
+
+    def key_grad(step, half, i):
+        if i == 0:
+            scores = (own_scores, next_scores)[half]
+            return dot(scores[step], qs[half].reshape(HEADS * ROWS, DIM), NN)
+        return dot(weights[...], gs[half].reshape(HEADS * ROWS, DIM), NN)
 
     def own_tile(step):
-        grad_k, grad_v = tile(step, 0, own_scores)
-        acc[step, 0] = grad_k
-        acc[step, 1] = grad_v
-
-    def query_grads(scores):
-        total = jnp.zeros((HEADS * ROWS, DIM), jnp.float32)
-        for step in range(Y_DEVICES):
-            total = total + dot(scores[step], kv[lax.rem(y + step, Y_DEVICES), 0], TN)
-        return total * inv_root
+        tile(step, 0, own_scores)
+        for i in (0, 1):
+            acc[step, i] = key_grad(step, 0, i)
+
+    def query_grads(scores, steps):
+        total = None
+        for step in steps:
+            part = dot(scores[step], kv[lax.rem(y + step, Y_DEVICES), 0], TN)
+            total = part if total is None else total + part
+        return total
 
     def pass_on(step):
-        wait_block(x, lax.rem(y + step, Y_DEVICES))
-        for distance in (1, 3, 2):
-            send_x(step, distance).start()
+        for i in (0, 1):
+            wait_block(x, lax.rem(y + step, Y_DEVICES), i)
+            for distance in (1, 3, 2):
+                send_x(step, distance, i).start()
 
     def wait_others(step):
-        for distance in (1, 3, 2):
-            wait_block(lax.rem(x + distance, X_DEVICES), lax.rem(y + step, Y_DEVICES))
+        for i in (0, 1):
+            for distance in (1, 3, 2):
+                wait_block(lax.rem(x + distance, X_DEVICES), lax.rem(y + step, Y_DEVICES), i)
+
+    def rs_x(step, distance, i):
+        xi = lax.rem(x + distance, X_DEVICES)
+        return pltpu.make_async_remote_copy(
+            sx.at[step, i, rows_of(xi), :], rx.at[step, distance - 1, i],
+            rs_send_x.at[step, distance - 1, i], rs_recv_x.at[step, distance - 1, i],
+            device_id=at_x(distance), device_id_type=MESH,
+        )
+
+    def rs_y(step, i):
+        return pltpu.make_async_remote_copy(
+            sy.at[step - 1, i], ry.at[step - 1, i], rs_send_y.at[step - 1, i],
+            rs_recv_y.at[step - 1, i], device_id=at_y(step), device_id_type=MESH,
+        )
+
+    def next_tile(step):
+        tile(step, 1, next_scores)
+        for i in (0, 1):
+            grad = acc[step, i] + key_grad(step, 1, i)
+            if i == 0:
+                grad = grad * inv_root
+            acc[step, i] = grad
+            sx[step, i] = grad.astype(jnp.bfloat16)
+            for distance in (2, 1, 3):
+                rs_x(step, distance, i).start()
+
+    def over_x(step, i):
+        total = acc[step, i, rows_of(x), :]
+        for distance in (1, 2, 3):
+            rs_x(step, distance, i).wait_recv()
+            total = total + rx[step, distance - 1, i].astype(jnp.float32)
+        return total
+
+    def to_y(step):
+        for i in (0, 1):
+            sy[step - 1, i] = over_x(step, i).astype(jnp.bfloat16)
+            rs_y(step, i).start()
+
+    def dq_copy(distance):
+        return pltpu.make_async_remote_copy(
+            sq, rq, dq_send, dq_recv, device_id=at_z(distance), device_id_type=MESH
+        )
+
+    def store(i):
+        return pltpu.make_async_copy(
+            (dq_out, dkv_out.at[0], dkv_out.at[1])[i], (dq_ref, dk_ref, dv_ref)[i],
+            local_sem.at[i],
+        )
 
     pass_on(1)
     pass_on(3)
     wait_others(0)
     own_tile(0)
     pass_on(2)
-    for step in (1, 3, 2):
-        wait_others(step)
-        own_tile(step)
+    wait_others(1)
+    own_tile(1)
 
     @pl.when(outer < OUTER - 1)
     def _():
@@ -222,88 +286,57 @@
         qs[1] = jnp.zeros_like(qs[1])
         gs[1] = jnp.zeros_like(gs[1])
 
-    def rs_x(step, distance):
-        xi = lax.rem(x + distance, X_DEVICES)
-        return pltpu.make_async_remote_copy(
-            sx.at[step, :, rows_of(xi), :], rx.at[step, distance - 1],
-            rs_send_x.at[step, distance - 1], rs_recv_x.at[step, distance - 1],
-            device_id=at_x(distance), device_id_type=MESH,
-        )
-
-    def rs_y(step):
-        return pltpu.make_async_remote_copy(
-            sy.at[step - 1], ry.at[step - 1], rs_send_y.at[step - 1],
-            rs_recv_y.at[step - 1], device_id=at_y(step), device_id_type=MESH,
-        )
-
-    def next_tile(step):
-        grad_k, grad_v = tile(step, 1, next_scores)
-        grad_k = (acc[step, 0] + grad_k) * inv_root
-        grad_v = acc[step, 1] + grad_v
-        acc[step, 0] = grad_k
-        acc[step, 1] = grad_v
-        sx[step, 0] = grad_k.astype(jnp.bfloat16)
-        sx[step, 1] = grad_v.astype(jnp.bfloat16)
-        for distance in (2, 1, 3):
-            rs_x(step, distance).start()
-
-    def over_x(step):
-        total = acc[step, :, rows_of(x), :]
+    next_tile(1)
+    wait_others(3)
+    own_tile(3)
+    wait_others(2)
+    own_tile(2)
+    next_tile(2)
+    next_tile(3)
+    to_y(1)
+    dq_next[...] = query_grads(next_scores, (2, 1, 3))
+    next_tile(0)
+    sq[...] = (
+        (dq_next[...] + query_grads(next_scores, (0,))) * inv_root
+    ).astype(jnp.bfloat16)
+
+    @pl.when(outer < OUTER - 1)
+    def _():
+        dq_copy(1).start()
+
+    to_y(2)
+    to_y(3)
+    totals = [over_x(0, 0), over_x(0, 1)]
+    own = query_grads(own_scores, range(Y_DEVICES)) * inv_root
+
+    @pl.when(outer > 0)
+    def _():
+        dq_copy(-1).wait_recv()
+
+    @pl.when(outer == 0)
+    def _():
+        rq[...] = jnp.zeros_like(rq)
+
+    dq_out[...] = (
+        (own + rq[...].astype(jnp.float32)).astype(jnp.bfloat16).reshape(HEADS, ROWS, DIM)
+    )
+    store(0).start()
+
+    for i in (0, 1):
+        total = totals[i]
+        for step in (1, 3, 2):
+            rs_y(step, i).wait_recv()
+            total = total + ry[step - 1, i].astype(jnp.float32)
+        dkv_out[i] = total.astype(jnp.bfloat16)
+        store(1 + i).start()
+
+    for i in (0, 1):
         for distance in (1, 2, 3):
-            rs_x(step, distance).wait_recv()
-            total = total + rx[step, distance - 1].astype(jnp.float32)
-        return total
-
-    def to_y(step):
-        sy[step - 1] = over_x(step).astype(jnp.bfloat16)
-        rs_y(step).start()
-
-    next_tile(2)
-    next_tile(1)
-    next_tile(3)
-    to_y(2)
-    next_tile(0)
-    to_y(1)
-
-    def dq_copy(distance):
-        return pltpu.make_async_remote_copy(
-            sq, rq, dq_send, dq_recv, device_id=at_z(distance), device_id_type=MESH
-        )
-
-    sq[...] = query_grads(next_scores).astype(jnp.bfloat16)
-
-    @pl.when(outer < OUTER - 1)
-    def _():
-        dq_copy(1).start()
-
-    to_y(3)
-    total = over_x(0)
-    own = query_grads(own_scores)
-
-    @pl.when(outer > 0)
-    def _():
-        dq_copy(-1).wait_recv()
-
-    @pl.when(outer == 0)
-    def _():
-        rq[...] = jnp.zeros_like(rq)
-
-    dq_ref[...] = (
-        (own + rq[...].astype(jnp.float32)).astype(jnp.bfloat16).reshape(HEADS, ROWS, DIM)
-    )
-
-    for step in (1, 2, 3):
-        rs_y(step).wait_recv()
-        total = total + ry[step - 1].astype(jnp.float32)
-    dk_ref[...] = total[0].astype(jnp.bfloat16)
-    dv_ref[...] = total[1].astype(jnp.bfloat16)
-
-    for distance in (1, 2, 3):
-        send_y(distance).wait_send()
-        rs_y(distance).wait_send()
-        for step in range(Y_DEVICES):
-            send_x(step, distance).wait_send()
-            rs_x(step, distance).wait_send()
+            send_y(distance, i).wait_send()
+            rs_y(distance, i).wait_send()
+            for step in range(Y_DEVICES):
+                send_x(step, distance, i).wait_send()
+                rs_x(step, distance, i).wait_send()
 
     @pl.when(outer > 0)
     def _():
@@ -313,6 +346,9 @@
     @pl.when(outer < OUTER - 1)
     def _():
         dq_copy(1).wait_send()
+
+    for i in range(3):
+        store(i).wait()
 
 
 def store_kernel(dq_in, dk_in, dv_in, dq_ref, dk_ref, dv_ref, sems):
@@ -345,7 +381,7 @@
         kernel,
         out_shape=grads,
         in_specs=[pl.BlockSpec(memory_space=pltpu.SMEM), hbm, hbm, hbm, hbm, hbm, hbm],
-        out_specs=(vmem, vmem, vmem),
+        out_specs=(hbm, hbm, hbm),
         scratch_shapes=[
             pltpu.VMEM((Y_DEVICES, 2, GROUP_KEYS, DIM), half),
             pltpu.VMEM((2, HEADS, ROWS, DIM), half),
@@ -358,14 +394,17 @@
             pltpu.VMEM((Y_DEVICES, GROUP_KEYS, HEADS * ROWS), half),
             pltpu.VMEM((Y_DEVICES, GROUP_KEYS, HEADS * ROWS), half),
             pltpu.VMEM((Y_DEVICES, 2, GROUP_KEYS, DIM), full),
+            pltpu.VMEM((HEADS * ROWS, DIM), full),
             pltpu.VMEM((Y_DEVICES, 2, GROUP_KEYS, DIM), half),
             pltpu.VMEM((Y_DEVICES, 3, 2, ROWS, DIM), half),
             pltpu.VMEM((3, 2, ROWS, DIM), half),
             pltpu.VMEM((3, 2, ROWS, DIM), half),
             pltpu.VMEM((HEADS * ROWS, DIM), half),
             pltpu.VMEM((HEADS * ROWS, DIM), half),
-            dma((6,)), dma((3,)), dma((3,)), dma((3,)), dma((4, 3)), dma((16,)),
-            dma((4, 3)), dma((4, 3)), dma((3,)), dma((3,)), dma, dma,
+            pltpu.VMEM((HEADS, ROWS, DIM), half),
+            pltpu.VMEM((2, ROWS, DIM), half),
+            dma((6,)), dma((3,)), dma((3,)), dma((3, 2)), dma((3, 2)), dma((3, 3, 2)),
+            dma((16, 2)), dma((4, 3, 2)), dma((4, 3, 2)), dma((3, 2)), dma((3, 2)), dma, dma,
         ],
         compiler_params=pltpu.CompilerParams(
             collective_id=0, has_side_effects=True, vmem_limit_bytes=60 * 2**20

time: 45.5 us -> 42.9 us (0.943)
  the two profiles are of different devices: /device:TPU:390 before, /device:TPU:192 now
where the time goes in v3:
time: 42.9 us; the launch traced here: 42.7 us
  Pallas kernels  42 us (98%)
  between operations  0.64 us (1%)
    pallas_call x1, Pallas kernels, on_device(): pl.pallas_call(kernel, out_shape=grads, in_specs=[pl.BlockSpec(memory_spa...  40.4 us
    pallas_call x1, Pallas kernels, on_device(): pl.pallas_call(store_kernel, out_shape=grads, in_specs=[vmem, vmem, vmem]...  1.67 us

profile of v3, /device:TPU:192, one launch (start us, length us, event | category | flops | bytes accessed | tf_op | source)
XLA Modules:
  0.0 42.7 jit_solution(11103957582904027315)
XLA Ops:
  0.6 40.4 %shard_map.94 = (bf16[6,128,128]{2,1,0:T(8,128)(2,1)}, bf16[128,128]{1,0:T(8,128)(2,1)}, bf16[128,128]{1,0:T(8,128)(2,1)}) custom-call(s32[16]{0:T(128)} %order_ref.1, bf16[6,128,128]{2,1,0:T(8,128)(2,1)} %bitcast.8, bf16[128,128]{1,0:T(8,128)(2,1)} %bitcast.12, bf16[128,128]{1,0:T(8,128)(2,1)} %bitcast.13, bf16[6,128,128]{2,1,0:T(8,128)(2,1)} %bitcast.9, ...), custom_call_target="tpu_custom_call" | custom-call | flops 4000000000 | bytes 1000000 | tf_op jit(solution)/shard_map/pallas_call | solution.py:380
  41.0 1.7 %shard_map.95 = (bf16[6,128,128]{2,1,0:T(8,128)(2,1)}, bf16[128,128]{1,0:T(8,128)(2,1)}, bf16[128,128]{1,0:T(8,128)(2,1)}) custom-call(bf16[6,128,128]{2,1,0:T(8,128)(2,1)} %get-tuple-element.9.dq_in, bf16[128,128]{1,0:T(8,128)(2,1)} %get-tuple-element.10.dk_in, bf16[128,128]{1,0:T(8,128)(2,1)} %get-tuple-element.11.dv_in), custom_call_target="tpu_custom_call" | custom-call | tf_op jit(solution)/shard_map/pallas_call | solution.py:424

commit v4 on v3

--- a/solution.py
+++ b/solution.py
@@ -33,7 +33,7 @@
     order_ref, q_ref, k_ref, v_ref, o_ref, g_ref, lse_ref,
     dq_ref, dk_ref, dv_ref,
     kv, qs, gs, attn, lse, stat, kpos, weights, own_scores, next_scores, acc, dq_next,
-    sx, rx, sy, ry, sq, rq, dq_out, dkv_out,
+    sx, rx, sy, ry, sq, rq,
     local_sem, z_send, z_recv, ag_send_y, ag_send_own, ag_send_x, ag_recv,
     rs_send_x, rs_recv_x, rs_send_y, rs_recv_y, dq_send, dq_recv,
 ):
@@ -261,12 +261,6 @@
             sq, rq, dq_send, dq_recv, device_id=at_z(distance), device_id_type=MESH
         )
 
-    def store(i):
-        return pltpu.make_async_copy(
-            (dq_out, dkv_out.at[0], dkv_out.at[1])[i], (dq_ref, dk_ref, dv_ref)[i],
-            local_sem.at[i],
-        )
-
     pass_on(1)
     pass_on(3)
     wait_others(0)
@@ -317,18 +311,16 @@
     def _():
         rq[...] = jnp.zeros_like(rq)
 
-    dq_out[...] = (
+    dq_ref[...] = (
         (own + rq[...].astype(jnp.float32)).astype(jnp.bfloat16).reshape(HEADS, ROWS, DIM)
     )
-    store(0).start()
 
     for i in (0, 1):
         total = totals[i]
         for step in (1, 3, 2):
             rs_y(step, i).wait_recv()
             total = total + ry[step - 1, i].astype(jnp.float32)
-        dkv_out[i] = total.astype(jnp.bfloat16)
-        store(1 + i).start()
+        (dk_ref, dv_ref)[i][...] = total.astype(jnp.bfloat16)
 
     for i in (0, 1):
         for distance in (1, 2, 3):
@@ -346,9 +338,6 @@
     @pl.when(outer < OUTER - 1)
     def _():
         dq_copy(1).wait_send()
-
-    for i in range(3):
-        store(i).wait()
 
 
 def store_kernel(dq_in, dk_in, dv_in, dq_ref, dk_ref, dv_ref, sems):
@@ -379,9 +368,9 @@
     )
     parts = pl.pallas_call(
         kernel,
-        out_shape=grads,
+        out_shape=tuple(pltpu.VMEM(grad.shape, grad.dtype) for grad in grads),
         in_specs=[pl.BlockSpec(memory_space=pltpu.SMEM), hbm, hbm, hbm, hbm, hbm, hbm],
-        out_specs=(hbm, hbm, hbm),
+        out_specs=(vmem, vmem, vmem),
         scratch_shapes=[
             pltpu.VMEM((Y_DEVICES, 2, GROUP_KEYS, DIM), half),
             pltpu.VMEM((2, HEADS, ROWS, DIM), half),
@@ -401,8 +390,6 @@
             pltpu.VMEM((3, 2, ROWS, DIM), half),
             pltpu.VMEM((HEADS * ROWS, DIM), half),
             pltpu.VMEM((HEADS * ROWS, DIM), half),
-            pltpu.VMEM((HEADS, ROWS, DIM), half),
-            pltpu.VMEM((2, ROWS, DIM), half),
             dma((6,)), dma((3,)), dma((3,)), dma((3, 2)), dma((3, 2)), dma((3, 3, 2)),
             dma((16, 2)), dma((4, 3, 2)), dma((4, 3, 2)), dma((3, 2)), dma((3, 2)), dma, dma,
         ],
@@ -427,6 +414,7 @@
         in_specs=[vmem, vmem, vmem],
         out_specs=(hbm, hbm, hbm),
         scratch_shapes=[dma((3,))],
+        compiler_params=pltpu.CompilerParams(vmem_limit_bytes=2**20),
     )(*parts)
     return (
         jnp.transpose(grad_queries, (1, 0, 2)),

time: 42.9 us -> 41.4 us (0.965)
  Pallas kernels: 42 us -> 40.6 us
    pallas_call x1, Pallas kernels: 1.67 us -> 0.72 us  [on_device(): pl.pallas_call(store_kernel, out_shape=grads, in_specs=[vmem, vmem, vmem]...]
    pallas_call x1, Pallas kernels: 40.4 us -> 39.9 us  [on_device(): pl.pallas_call(kernel, out_shape=tuple((pltpu.VMEM(grad.shape, grad.dtype...]
where the time goes in v4:
time: 41.4 us; the launch traced here: 41.2 us
  Pallas kernels  40.6 us (98%)
  between operations  0.64 us (2%)
    pallas_call x1, Pallas kernels, on_device(): pl.pallas_call(kernel, out_shape=tuple((pltpu.VMEM(grad.shape, grad.dtype...  39.9 us

profile of v4, /device:TPU:192, one launch (start us, length us, event | category | flops | bytes accessed | tf_op | source)
XLA Modules:
  0.0 41.2 jit_solution(7017004118482027124)
XLA Ops:
  0.6 39.9 %shard_map.94 = (bf16[6,128,128]{2,1,0:T(8,128)(2,1)S(1)}, bf16[128,128]{1,0:T(8,128)(2,1)S(1)}, bf16[128,128]{1,0:T(8,128)(2,1)S(1)}) custom-call(s32[16]{0:T(128)} %order_ref.1, bf16[6,128,128]{2,1,0:T(8,128)(2,1)} %bitcast.8, bf16[128,128]{1,0:T(8,128)(2,1)} %bitcast.12, bf16[128,128]{1,0:T(8,128)(2,1)} %bitcast.13, bf16[6,128,128]{2,1,0:T(8,128)(2,1)} %bitcast.9, ...), custom_call_target="tpu_custom_call" | custom-call | flops 4000000000 | bytes 1000000 | tf_op jit(solution)/shard_map/pallas_call | solution.py:369
  40.5 0.7 %shard_map.95 = (bf16[6,128,128]{2,1,0:T(8,128)(2,1)}, bf16[128,128]{1,0:T(8,128)(2,1)}, bf16[128,128]{1,0:T(8,128)(2,1)}) custom-call(bf16[6,128,128]{2,1,0:T(8,128)(2,1)S(1)} %get-tuple-element.9.dq_in, bf16[128,128]{1,0:T(8,128)(2,1)S(1)} %get-tuple-element.10.dk_in, bf16[128,128]{1,0:T(8,128)(2,1)S(1)} %get-tuple-element.11.dv_in), custom_call_target="tpu_custom_call" | custom-call | tf_op jit(solution)/shard_map/pallas_call | solution.py:411

commit v5 on v4

--- a/solution.py
+++ b/solution.py
@@ -59,6 +59,19 @@
     def block(xi, yi, i):
         return kv.at[yi, i, rows_of(xi), :]
 
+    barrier = pltpu.get_barrier_semaphore()
+    for distance in (1, 2, 3):
+        pl.semaphore_signal(barrier, inc=1, device_id=at_x(distance), device_id_type=MESH)
+        pl.semaphore_signal(barrier, inc=1, device_id=at_y(distance), device_id_type=MESH)
+
+    @pl.when(outer > 0)
+    def _():
+        pl.semaphore_signal(barrier, inc=1, device_id=at_z(-1), device_id_type=MESH)
+
+    @pl.when(outer < OUTER - 1)
+    def _():
+        pl.semaphore_signal(barrier, inc=1, device_id=at_z(1), device_id_type=MESH)
+
     loads = [
         pltpu.make_async_copy(k_ref, kv.at[y, 0, rows_of(x), :], local_sem.at[0]),
         pltpu.make_async_copy(v_ref, kv.at[y, 1, rows_of(x), :], local_sem.at[1]),
@@ -70,19 +83,6 @@
     for load in loads:
         load.start()
 
-    barrier = pltpu.get_barrier_semaphore()
-    for distance in (1, 2, 3):
-        pl.semaphore_signal(barrier, inc=1, device_id=at_x(distance), device_id_type=MESH)
-        pl.semaphore_signal(barrier, inc=1, device_id=at_y(distance), device_id_type=MESH)
-
-    @pl.when(outer > 0)
-    def _():
-        pl.semaphore_signal(barrier, inc=1, device_id=at_z(-1), device_id_type=MESH)
-
-    @pl.when(outer < OUTER - 1)
-    def _():
-        pl.semaphore_signal(barrier, inc=1, device_id=at_z(1), device_id_type=MESH)
-
     peers = 6 + jnp.minimum(outer, 1) + jnp.minimum(OUTER - 1 - outer, 1)
     pl.semaphore_wait(barrier, peers)
 
@@ -124,8 +124,8 @@
         for copy in z_copies()[:2]:
             copy.start()
 
-    for i in (0, 1):
-        for distance in (1, 3, 2):
+    for distance in (1, 3, 2):
+        for i in (0, 1):
             send_y(distance, i).start()
 
     for i in (0, 1):
@@ -233,7 +233,12 @@
             rs_recv_y.at[step - 1, i], device_id=at_y(step), device_id_type=MESH,
         )
 
-    def next_tile(step):
+    def send_tile(step):
+        for i in (0, 1):
+            for distance in (2, 1, 3):
+                rs_x(step, distance, i).start()
+
+    def next_tile(step, send=True):
         tile(step, 1, next_scores)
         for i in (0, 1):
             grad = acc[step, i] + key_grad(step, 1, i)
@@ -241,8 +246,9 @@
                 grad = grad * inv_root
             acc[step, i] = grad
             sx[step, i] = grad.astype(jnp.bfloat16)
-            for distance in (2, 1, 3):
-                rs_x(step, distance, i).start()
+            if send:
+                for distance in (2, 1, 3):
+                    rs_x(step, distance, i).start()
 
     def over_x(step, i):
         total = acc[step, i, rows_of(x), :]
@@ -283,10 +289,11 @@
     next_tile(1)
     wait_others(3)
     own_tile(3)
+    next_tile(3, False)
     wait_others(2)
     own_tile(2)
     next_tile(2)
-    next_tile(3)
+    send_tile(3)
     to_y(1)
     dq_next[...] = query_grads(next_scores, (2, 1, 3))
     next_tile(0)

time: 41.4 us -> 41 us (level)
  no operation moved by 1% of the time
where the time goes in v5:
time: 41 us; the launch traced here: 40.9 us
  Pallas kernels  40.2 us (98%)
  between operations  0.64 us (2%)
    pallas_call x1, Pallas kernels, on_device(): pl.pallas_call(kernel, out_shape=tuple((pltpu.VMEM(grad.shape, grad.dtype...  39.5 us

profile of v5, /device:TPU:192, one launch (start us, length us, event | category | flops | bytes accessed | tf_op | source)
XLA Modules:
  0.0 40.9 jit_solution(3879798572771487525)
XLA Ops:
  0.6 39.5 %shard_map.94 = (bf16[6,128,128]{2,1,0:T(8,128)(2,1)S(1)}, bf16[128,128]{1,0:T(8,128)(2,1)S(1)}, bf16[128,128]{1,0:T(8,128)(2,1)S(1)}) custom-call(s32[16]{0:T(128)} %order_ref.1, bf16[6,128,128]{2,1,0:T(8,128)(2,1)} %bitcast.8, bf16[128,128]{1,0:T(8,128)(2,1)} %bitcast.12, bf16[128,128]{1,0:T(8,128)(2,1)} %bitcast.13, bf16[6,128,128]{2,1,0:T(8,128)(2,1)} %bitcast.9, ...), custom_call_target="tpu_custom_call" | custom-call | flops 4000000000 | bytes 1000000 | tf_op jit(solution)/shard_map/pallas_call | solution.py:376
  40.1 0.7 %shard_map.95 = (bf16[6,128,128]{2,1,0:T(8,128)(2,1)}, bf16[128,128]{1,0:T(8,128)(2,1)}, bf16[128,128]{1,0:T(8,128)(2,1)}) custom-call(bf16[6,128,128]{2,1,0:T(8,128)(2,1)S(1)} %get-tuple-element.9.dq_in, bf16[128,128]{1,0:T(8,128)(2,1)S(1)} %get-tuple-element.10.dk_in, bf16[128,128]{1,0:T(8,128)(2,1)S(1)} %get-tuple-element.11.dv_in), custom_call_target="tpu_custom_call" | custom-call | tf_op jit(solution)/shard_map/pallas_call | solution.py:418

commit v6 on v5

--- a/solution.py
+++ b/solution.py
@@ -290,15 +290,15 @@
     wait_others(3)
     own_tile(3)
     next_tile(3, False)
+    dq_next[...] = query_grads(next_scores, (1, 3))
     wait_others(2)
     own_tile(2)
     next_tile(2)
     send_tile(3)
     to_y(1)
-    dq_next[...] = query_grads(next_scores, (2, 1, 3))
     next_tile(0)
     sq[...] = (
-        (dq_next[...] + query_grads(next_scores, (0,))) * inv_root
+        (dq_next[...] + query_grads(next_scores, (2, 0,))) * inv_root
     ).astype(jnp.bfloat16)
 
     @pl.when(outer < OUTER - 1)

time: 41 us -> 41.7 us (1.017)
  Pallas kernels: 40.2 us -> 40.9 us
    pallas_call x1, Pallas kernels: 39.5 us -> 40.2 us  [on_device(): pl.pallas_call(kernel, out_shape=tuple((pltpu.VMEM(grad.shape, grad.dtype...]
where the time goes in v6:
time: 41.7 us; the launch traced here: 41.6 us
  Pallas kernels  40.9 us (98%)
  between operations  0.64 us (2%)
    pallas_call x1, Pallas kernels, on_device(): pl.pallas_call(kernel, out_shape=tuple((pltpu.VMEM(grad.shape, grad.dtype...  40.2 us

profile of v6, /device:TPU:192, one launch (start us, length us, event | category | flops | bytes accessed | tf_op | source)
XLA Modules:
  0.0 41.6 jit_solution(6949628716681423031)
XLA Ops:
  0.6 40.2 %shard_map.94 = (bf16[6,128,128]{2,1,0:T(8,128)(2,1)S(1)}, bf16[128,128]{1,0:T(8,128)(2,1)S(1)}, bf16[128,128]{1,0:T(8,128)(2,1)S(1)}) custom-call(s32[16]{0:T(128)} %order_ref.1, bf16[6,128,128]{2,1,0:T(8,128)(2,1)} %bitcast.8, bf16[128,128]{1,0:T(8,128)(2,1)} %bitcast.12, bf16[128,128]{1,0:T(8,128)(2,1)} %bitcast.13, bf16[6,128,128]{2,1,0:T(8,128)(2,1)} %bitcast.9, ...), custom_call_target="tpu_custom_call" | custom-call | flops 4000000000 | bytes 1000000 | tf_op jit(solution)/shard_map/pallas_call | solution.py:376
  40.9 0.7 %shard_map.95 = (bf16[6,128,128]{2,1,0:T(8,128)(2,1)}, bf16[128,128]{1,0:T(8,128)(2,1)}, bf16[128,128]{1,0:T(8,128)(2,1)}) custom-call(bf16[6,128,128]{2,1,0:T(8,128)(2,1)S(1)} %get-tuple-element.9.dq_in, bf16[128,128]{1,0:T(8,128)(2,1)S(1)} %get-tuple-element.10.dk_in, bf16[128,128]{1,0:T(8,128)(2,1)S(1)} %get-tuple-element.11.dv_in), custom_call_target="tpu_custom_call" | custom-call | tf_op jit(solution)/shard_map/pallas_call | solution.py:418
